TPU v7x, 128 devices: a whole 4x4x4 slice. The times are simulated.
128 devices in a mesh: gx: 32 (over z, x, core), gy: 4 (over y).
Axes of the slice: x: 4, y: 4, z: 4, core: 2. Of those that a mesh axis runs over, the one named last changes fastest.
Arguments:
- state: float32 [4, 1024, 512, 128], P(None, 'gx', 'gy'), may hold values from -6 to 6
- velocity: float32 [3, 1024, 512, 128], P(None, 'gx', 'gy'), may hold values from -6 to 6
- threshold: float32 [32, 512], P('gx', 'gy'), may hold values from 0.5 to 3
- tile_owner: int32 [4, 1024, 1], P('gy', 'gx'), may hold values from 0 to 31; in each aligned block of 32 rows (0 to 31, 32 to 63, ..., all dimensions but the last counted through in order) at most 2 rows name the same one
- parcel_owner: int32 [4, 1024, 1], P('gy', 'gx'), may hold values from 0 to 31; in each aligned block of 32 rows (0 to 31, 32 to 63, ..., all dimensions but the last counted through in order) at most 2 rows name the same one
- parcel_count: int32 [4, 1024], P('gy', 'gx'), may hold values from 1 to 128, as said below
- parcel_share: float32 [4, 1024, 128], P('gy', 'gx'), may hold values from 0.2 to 1
Outputs:
- fields: float32 [4, 1024, 512, 128], P(None, 'gx', 'gy')
- ground_flux: float32 [32, 512], P('gx', 'gy')
Inputs may be any that keep to these rules, and one draw needn't show every extreme that they name: `tile_owner`: among the 32 tiles of one device no owner is named more than 2 times, and that count is reached. `parcel_owner`: among the 32 rows of one owner no destination is named more than 2 times, and that count is reached. `parcel_count`: the first row of every owner has 128 live parcels.
All inputs are finite; a program needn't handle non-finite values.
Results may differ from a plain program's by a relative error of at most 0.0003.
Values sent between devices are 32-bit elements; how exact they have to be, the bound alone decides.
A program may use at most 256 MiB of HBM per device.

v0:
```python
import jax
import jax.numpy as jnp
from jax import lax
from jax.sharding import PartitionSpec as P

LEVELS = 4
STEPS = 2


profile_weights = (0.4, 0.3, 0.2, 0.1)
time_step = 0.1


def extended(block, sides, width):
    for axis, dim in sides:
        count = lax.axis_size(axis)
        forward = [(i, i + 1) for i in range(count - 1)]
        backward = [(target, source) for source, target in forward]
        low = lax.ppermute(
            lax.slice_in_dim(block, block.shape[dim] - width, None, axis=dim), axis, forward
        )
        high = lax.ppermute(lax.slice_in_dim(block, 0, width, axis=dim), axis, backward)
        block = jnp.concatenate([low, block, high], axis=dim)
    return block


def friction(east, north):
    total = profile_weights[0] * (
        east[..., 0, :] * east[..., 0, :] + north[..., 0, :] * north[..., 0, :]
    )
    for level in range(1, east.shape[-2]):
        total = total + profile_weights[level] * (
            east[..., level, :] * east[..., level, :] + north[..., level, :] * north[..., level, :]
        )
    return total


def minmod(first, second):
    return jnp.where(
        first * second > 0, jnp.sign(first) * jnp.minimum(jnp.abs(first), jnp.abs(second)), 0.0
    )


def section(array, axis, start, stop):
    return lax.slice_in_dim(array, start, stop, axis=axis)


def divergence(field, speed, axis):
    count = field.shape[axis] - 4
    behind = section(field, axis, 0, count + 1)
    here = section(field, axis, 1, count + 2)
    ahead = section(field, axis, 2, count + 3)
    beyond = section(field, axis, 3, count + 4)
    face_speed = 0.5 * (section(speed, axis, 1, count + 2) + section(speed, axis, 2, count + 3))
    upwind = face_speed * (here + 0.5 * minmod(ahead - here, here - behind))
    downwind = face_speed * (ahead - 0.5 * minmod(beyond - ahead, ahead - here))
    fluxes = jnp.where(face_speed > 0, upwind, downwind)
    return section(fluxes, axis, 1, count + 1) - section(fluxes, axis, 0, count)


def advance(padded, wind):
    inner = padded[:, 2:-2, 2:-2, 2:-2]
    along_x = divergence(padded[:, :, 2:-2, 2:-2], wind[0:1, :, 2:-2, 2:-2], 1)
    along_y = divergence(padded[:, 2:-2, :, 2:-2], wind[1:2, 2:-2, :, 2:-2], 2)
    along_z = divergence(padded[:, 2:-2, 2:-2, :], wind[2:3, 2:-2, 2:-2, :], 3)
    return inner - time_step * (along_x + along_y + along_z)


def vertical_pad(array):
    return jnp.pad(array, ((0, 0), (0, 0), (0, 0), (2, 2)))


def pack_slots(targets, payload, groups, capacity):
    count = targets.shape[0]
    same = targets[:, None] == targets[None, :]
    earlier = jnp.arange(count)[None, :] < jnp.arange(count)[:, None]
    ranking = jnp.sum((same & earlier).astype(jnp.int32), axis=1)
    slot_index = targets * capacity + ranking
    placing = (slot_index[None, :] == jnp.arange(groups * capacity)[:, None]).astype(jnp.float32)
    return jnp.dot(placing, payload, precision=lax.Precision.HIGHEST)


def transport_all(fields, wind):
    for substep in range(STEPS):
        padded = extended(fields, (("gx", 1), ("gy", 2)), 2)
        fields = advance(vertical_pad(padded), wind)
    return fields


def shards(state, velocity, threshold, tile_owner, parcel_owner, parcel_count, parcel_share):
    groups = lax.axis_size("gx")
    rows_x = state.shape[1]
    width_y = state.shape[2]
    tile_slots = max(2, 2 * rows_x // groups)
    row_slots = max(2, 2 * parcel_owner.shape[1] // groups)
    wind = vertical_pad(extended(velocity, (("gx", 1), ("gy", 2)), 2))
    east = velocity[0, :, :, 0:LEVELS].transpose(0, 2, 1)
    north = velocity[1, :, :, 0:LEVELS].transpose(0, 2, 1)
    targets = tile_owner[0, :, 0]
    payload = jnp.stack([east, north], axis=1).reshape(rows_x, 2 * LEVELS * width_y)
    packed = pack_slots(targets, payload, groups, tile_slots).reshape(
        groups, tile_slots, 2, LEVELS, width_y
    )
    arrived = lax.all_to_all(packed, "gx", split_axis=0, concat_axis=0, tiled=True)
    stress = friction(arrived[:, :, 0], arrived[:, :, 1])
    lifting = jnp.maximum(stress - threshold[0][None, None, :], 0.0)
    flux = jnp.sum(lifting, axis=(0, 1)) / rows_x
    reach = (jnp.arange(width_y)[None, :] < parcel_count[0][:, None]).astype(jnp.float32)
    masses = flux[None, :] * parcel_share[0] * reach
    packed_rows = pack_slots(parcel_owner[0, :, 0], masses, groups, row_slots).reshape(
        groups, row_slots, width_y
    )
    landed = lax.all_to_all(packed_rows, "gx", split_axis=0, concat_axis=0, tiled=True)
    per_source = jnp.sum(landed, axis=1)
    landing = (jnp.arange(groups)[None, :] % rows_x == jnp.arange(rows_x)[:, None]).astype(
        jnp.float32
    )
    deposit = jnp.dot(landing, per_source, precision=lax.Precision.HIGHEST)
    dust = state[3:4].at[0, :, :, 0].add(deposit)
    fields = transport_all(jnp.concatenate([state[0:3], dust], axis=0), wind)
    return (fields, flux[None, :])


def solution(mesh):
    return jax.shard_map(
        shards,
        mesh=mesh,
        in_specs=(
            P(None, "gx", "gy", None),
            P(None, "gx", "gy", None),
            P("gx", "gy"),
            P("gy", "gx", None),
            P("gy", "gx", None),
            P("gy", "gx"),
            P("gy", "gx", None),
        ),
        out_specs=(P(None, "gx", "gy", None), P("gx", "gy")),
        check_vma=False,
    )
```

profile of v0, /device:TPU:32, one launch (start us, length us, event | category | flops | bytes accessed | tf_op | source)
XLA Modules:
  0.0 395.6 jit_solution(5970060699203751973)
XLA Ops:
  9.1 8.0 %all-to-all-start = ((f32[32,2,2,4,128]{4,3,2,1,0:T(4,128)}), f32[32,2,2,4,128]{4,3,2,1,0:T(4,128)S(1)}, u32[]{:S(2)}, u32[]{:S(2)}) async-start(f32[32,2,2,4,128]{4,3,2,1,0:T(4,128)} %copy.81), calls=%async_computation | async-start | bytes 524288 | tf_op jit(solution)/shard_map/all_to_all | solution.py:104
  21.3 5.6 %collective-permute-start.1 = (f32[3,2,128,128]{3,2,1,0:T(8,128)}, f32[3,2,128,128]{3,2,1,0:T(8,128)S(1)}, u32[]{:S(2)}, u32[]{:S(2)}) collective-permute-start(f32[3,2,128,128]{3,2,1,0:T(8,128)} %get-tuple-element.36), channel_id=1, source_target_pairs={{4,0},{8,4},{12,8},{16,12},{20,16},{24,20},{28,24},{32,28},{36,32}... | collective-permute-start | bytes 1179656 | tf_op jit(solution)/shard_map/ppermute | solution.py:22
  28.6 5.3 %all-to-all-start.1 = ((f32[32,2,128]{2,1,0:T(2,128)}), f32[32,2,128]{2,1,0:T(2,128)S(1)}, u32[]{:S(2)}, u32[]{:S(2)}) async-start(f32[32,2,128]{2,1,0:T(2,128)} %copy.84), calls=%async_computation.1 | async-start | bytes 65536 | tf_op jit(solution)/shard_map/all_to_all | solution.py:113
  37.1 6.4 %slice.320 = f32[3,32,128,128]{3,2,1,0:T(8,128)} slice(f32[4,32,128,128]{3,2,1,0:T(8,128)} %param.9), slice={[0:3], [0:32], [0:128], [0:128]} | slice | bytes 12582912 | tf_op jit(solution)/shard_map/slice | solution.py:120
  47.9 5.4 %scatter-add.4 = f32[1,32,128,128]{3,2,1,0:T(8,128)S(1)} dynamic-update-slice(f32[1,32,128,128]{3,2,1,0:T(8,128)S(1)} %slice-done.4, f32[1,32,128,1]{3,2,1,0:T(8,128)} %copy.85, s32[]{:T(128)} %constant.70.clone.1, s32[]{:T(128)} %constant.70.clone.1, s32[]{:T(128)} %constant.70.clone.1, s32[]{:T(128)} %constant.70.clone.1) | dynamic-update-slice | bytes 32772 | tf_op jit(solution)/shard_map/scatter-add | solution.py:119
  56.1 4.6 %collective-permute-start.3 = (f32[4,2,128,128]{3,2,1,0:T(8,128)}, f32[4,2,128,128]{3,2,1,0:T(8,128)S(1)}, u32[]{:S(2)}, u32[]{:S(2)}) collective-permute-start(f32[4,2,128,128]{3,2,1,0:T(8,128)} %get-tuple-element.33), channel_id=1, source_target_pairs={{4,0},{8,4},{12,8},{16,12},{20,16},{24,20},{28,24},{32,28},{36,32}... | collective-permute-start | bytes 1572872 | tf_op jit(solution)/shard_map/ppermute | solution.py:22
  67.8 4.8 %collective-permute-start.4 = (f32[3,36,2,128]{3,2,1,0:T(2,128)S(1)}, f32[3,36,2,128]{3,2,1,0:T(2,128)S(1)}, u32[]{:S(2)}, u32[]{:S(2)}) collective-permute-start(f32[3,36,2,128]{3,2,1,0:T(2,128)S(1)} %get-tuple-element.34), channel_id=1, source_target_pairs={{0,1},{1,2},{2,3},{4,5},{5,6},{6,7},{8,9},{9,10},{10,11},{12,13},{... | collective-permute-start | bytes 331784 | tf_op jit(solution)/shard_map/ppermute | solution.py:19
  74.7 6.4 %select_maximum_fusion.9 = f32[3,36,132,132]{3,2,1,0:T(8,128)S(1)} fusion(f32[3,36,2,128]{3,2,1,0:T(2,128)S(1)} %collective-permute-done.5, f32[3,36,128,128]{3,2,1,0:T(8,128)S(1)} %constant_dynamic-update-slice_fusion, f32[3,36,2,128]{3,2,1,0:T(2,128)S(1)} %collective-permute-done.4), kind=kLoop, calls=%fused_computation.26 | loop fusion | flops 15054336 | bytes 14826240 | tf_op jit(solution)/shard_map/concatenate | solution.py:23
  94.5 6.0 %collective-permute-start.6 = (f32[4,36,2,128]{3,1,2,0:T(8,128)S(1)}, f32[4,36,2,128]{3,1,2,0:T(8,128)}, u32[]{:S(2)}, u32[]{:S(2)}) collective-permute-start(f32[4,36,2,128]{3,1,2,0:T(8,128)S(1)} %copy.86), channel_id=1, source_target_pairs={{0,1},{1,2},{2,3},{4,5},{5,6},{6,7},{8,9},{9,10},{10,11},{12,13},{... | collective-permute-start | bytes 442376 | tf_op jit(solution)/shard_map/ppermute | solution.py:19
  100.5 8.1 %maximum_maximum_fusion.2 = (f32[4,34,128,128]{3,2,1,0:T(8,128)}, f32[4,34,128,128]{3,2,1,0:T(8,128)}) fusion(f32[1,32,128,128]{3,2,1,0:T(8,128)S(1)} %copy-done.2, f32[3,32,128,128]{3,2,1,0:T(8,128)S(1)} %bitcast.63, f32[4,2,128,128]{3,2,1,0:T(8,128)} %collective-permute-done.2, f32[4,2,128,128]{3,2,1,0:T(8,128)S(1)} %collective-permute-done.3), kind=kLoop, calls=%fused_computation.42 | loop fusion | flops 8912896 | bytes 27262976 | tf_op jit(solution)/shard_map/concatenate | solution.py:23
  108.6 19.6 %multiply_select_fusion.5 = f32[4,33,128,128]{3,2,1,0:T(8,128)} fusion(f32[4,34,128,128]{3,2,1,0:T(8,128)} %get-tuple-element.31, f32[4,34,128,128]{3,2,1,0:T(8,128)} %get-tuple-element.30, f32[33,128,128]{2,1,0:T(8,128)} %bitcast.68, pred[33,128,128]{2,1,0:T(8,128)(4,1)S(1)} %copy-done.12), kind=kLoop, calls=%fused_computation.68 | loop fusion | flops 54067200 | bytes 45957120 | tf_op jit(solution)/shard_map/jit(_where)/select_n | solution.py:57
  129.3 23.9 %select_maximum_fusion.4 = f32[4,36,132,132]{3,2,1,0:T(8,128)} fusion(f32[4,36,2,128]{3,2,1,0:T(2,128)S(1)} %copy.89, f32[4,36,2,128]{3,2,1,0:T(2,128)S(1)} %copy.87, f32[4,2,128,128]{3,2,1,0:T(8,128)S(1)} %collective-permute-done.3, f32[4,2,128,128]{3,2,1,0:T(8,128)} %collective-permute-done.2, f32[1,32,128,128]{3,2,1,0:T(8,128)S(1)} %copy-done.2, ...), kind=kLoop, calls=%fused_computation.8 | loop fusion | flops 35126784 | bytes 19768320 | tf_op jit(solution)/shard_map/concatenate | solution.py:23
  153.2 48.3 %multiply_select_fusion.1 = f32[4,32,128,129]{3,2,1,0:T(8,128)} fusion(f32[4,36,132,132]{3,2,1,0:T(8,128)} %select_maximum_fusion.4, f32[32,128,129]{2,1,0:T(8,128)} %fusion.26, pred[32,128,129]{2,1,0:T(8,128)(4,1)S(1)} %compare_bitcast_fusion), kind=kLoop, calls=%fused_computation.22 | loop fusion | flops 52838400 | bytes 44912640 | tf_op jit(solution)/shard_map/jit(_where)/select_n | solution.py:57
  201.6 11.3 %maximum_maximum_fusion = (f32[4,36,130,128]{3,2,1,0:T(8,128)}, f32[4,36,130,128]{3,2,1,0:T(8,128)}) fusion(f32[4,2,128,128]{3,2,1,0:T(8,128)S(1)} %collective-permute-done.3, f32[1,32,128,128]{3,2,1,0:T(8,128)} %copy-done.1, f32[3,32,128,128]{3,2,1,0:T(8,128)S(1)} %bitcast.63, f32[4,2,128,128]{3,2,1,0:T(8,128)} %collective-permute-done.2, ...), kind=kLoop, calls=%fused_computation.32 | loop fusion | flops 19169280 | bytes 28901376 | tf_op jit(solution)/shard_map/concatenate | solution.py:23
  212.9 19.3 %multiply_select_fusion.3 = f32[4,32,129,128]{3,2,1,0:T(8,128)} fusion(f32[4,36,130,128]{3,2,1,0:T(8,128)} %get-tuple-element.25, f32[4,36,130,128]{3,2,1,0:T(8,128)} %get-tuple-element.24, f32[32,129,128]{2,1,0:T(8,128)S(1)} %bitcast.66, pred[32,129,128]{2,1,0:T(8,128)(4,1)S(1)} %copy-done.10), kind=kLoop, calls=%fused_computation.52 | loop fusion | flops 52838400 | bytes 44912640 | tf_op jit(solution)/shard_map/jit(_where)/select_n | solution.py:57
  232.2 19.9 %fusion.12 = f32[4,32,128,128]{3,2,1,0:T(8,128)S(1)} fusion(f32[1,32,128,128]{3,2,1,0:T(8,128)S(1)} %copy-done.3, f32[3,32,128,128]{3,2,1,0:T(8,128)S(1)} %bitcast.63, f32[4,32,128,129]{3,2,1,0:T(8,128)} %multiply_select_fusion.1, f32[4,32,129,128]{3,2,1,0:T(8,128)} %multiply_select_fusion.3, f32[4,33,128,128]{3,2,1,0:T(8,128)} %multiply_select_fusion.5), kind=kLoop, calls=%fused_computation.72 | loop fusion | flops 16777216 | bytes 67108864 | tf_op jit(solution)/shard_map/sub | solution.py:66
  258.6 4.7 %collective-permute-done.9 = f32[4,2,128,128]{3,2,1,0:T(8,128)S(1)} collective-permute-done((f32[4,2,128,128]{3,2,1,0:T(8,128)S(1)}, f32[4,2,128,128]{3,2,1,0:T(8,128)S(1)}, u32[]{:S(2)}, u32[]{:S(2)}) %collective-permute-start.9) | collective-permute-done | bytes 524320 | tf_op jit(solution)/shard_map/ppermute | solution.py:22
  263.3 5.9 %collective-permute-done.8 = f32[4,2,128,128]{3,2,1,0:T(8,128)S(1)} collective-permute-done((f32[4,2,128,128]{3,2,1,0:T(8,128)S(1)}, f32[4,2,128,128]{3,2,1,0:T(8,128)S(1)}, u32[]{:S(2)}, u32[]{:S(2)}) %collective-permute-start.8) | collective-permute-done | bytes 524320 | tf_op jit(solution)/shard_map/ppermute | solution.py:19
  275.3 11.8 %multiply_select_fusion.4 = f32[4,33,128,128]{3,2,1,0:T(8,128)} fusion(f32[4,2,128,128]{3,2,1,0:T(8,128)S(1)} %collective-permute-done.9, f32[4,32,128,128]{3,2,1,0:T(8,128)S(1)} %fusion.12, f32[4,2,128,128]{3,2,1,0:T(8,128)S(1)} %collective-permute-done.8, f32[33,128,128]{2,1,0:T(8,128)S(1)} %bitcast.69, pred[33,128,128]{2,1,0:T(8,128)(4,1)S(1)} %copy-done.13), kind=kLoop, calls=%fused_computation.64 | loop fusion | flops 62717952 | bytes 20791296 | tf_op jit(solution)/shard_map/jit(_where)/select_n | solution.py:57
  287.4 18.0 %select_maximum_fusion = f32[4,36,132,132]{3,2,1,0:T(8,128)} fusion(f32[4,36,2,128]{3,2,1,0:T(2,128)S(1)} %copy.95, f32[4,36,2,128]{3,2,1,0:T(2,128)S(1)} %copy.93, f32[4,2,128,128]{3,2,1,0:T(8,128)S(1)} %collective-permute-done.9, f32[4,32,128,128]{3,2,1,0:T(8,128)S(1)} %fusion.12, f32[4,2,128,128]{3,2,1,0:T(8,128)S(1)} %collective-permute-done.8), kind=kLoop, calls=%fused_computation.4 | loop fusion | flops 30108672 | bytes 19768320 | tf_op jit(solution)/shard_map/concatenate | solution.py:23
  305.4 37.6 %multiply_select_fusion = f32[4,32,128,129]{3,2,1,0:T(8,128)} fusion(f32[4,36,132,132]{3,2,1,0:T(8,128)} %select_maximum_fusion, f32[32,128,129]{2,1,0:T(8,128)S(1)} %copy-done.4, pred[32,128,129]{2,1,0:T(8,128)(4,1)S(1)} %compare_bitcast_fusion), kind=kLoop, calls=%fused_computation.18 | loop fusion | flops 52838400 | bytes 44912640 | tf_op jit(solution)/shard_map/jit(_where)/select_n | solution.py:57
  343.0 11.9 %maximum_maximum_fusion.1 = (f32[4,36,130,128]{3,2,1,0:T(8,128)S(1)}, f32[4,36,130,128]{3,2,1,0:T(8,128)}) fusion(f32[4,2,128,128]{3,2,1,0:T(8,128)S(1)} %collective-permute-done.9, f32[4,32,128,128]{3,2,1,0:T(8,128)} %copy-done, f32[4,2,128,128]{3,2,1,0:T(8,128)} %copy-done.9, f32[4,36,2,128]{3,2,1,0:T(2,128)S(1)} %copy.93, f32[4,36,2,128]{3,2,1,0:T(2,128)S(1)} %copy.95), kind=kLoop, calls=%fused_computation.34 | loop fusion | flops 14376960 | bytes 28901376 | tf_op jit(solution)/shard_map/concatenate | solution.py:23
  354.9 17.0 %multiply_select_fusion.2 = f32[4,32,129,128]{3,2,1,0:T(8,128)} fusion(f32[4,36,130,128]{3,2,1,0:T(8,128)} %get-tuple-element.21, f32[4,36,130,128]{3,2,1,0:T(8,128)S(1)} %get-tuple-element.20, f32[32,129,128]{2,1,0:T(8,128)S(1)} %bitcast.67, pred[32,129,128]{2,1,0:T(8,128)(4,1)S(1)} %copy-done.11), kind=kLoop, calls=%fused_computation.48 | loop fusion | flops 52838400 | bytes 44912640 | tf_op jit(solution)/shard_map/jit(_where)/select_n | solution.py:57
  371.9 23.3 %fusion.15 = f32[4,32,128,128]{3,2,1,0:T(8,128)} fusion(f32[4,32,128,128]{3,2,1,0:T(8,128)S(1)} %bitcast.61, f32[4,32,128,129]{3,2,1,0:T(8,128)} %multiply_select_fusion, f32[4,32,129,128]{3,2,1,0:T(8,128)} %multiply_select_fusion.2, f32[4,33,128,128]{3,2,1,0:T(8,128)} %multiply_select_fusion.4), kind=kLoop, calls=%fused_computation.76 | loop fusion | flops 14680064 | bytes 67108864 | tf_op jit(solution)/shard_map/sub | solution.py:66
  (122 shorter events, 60.6 us)
Async XLA Ops:
  0.6 26.3 %copy-start.17 = (s32[1,32,1]{1,2,0:T(1,128)S(1)}, s32[1,32,1]{1,2,0:T(1,128)}, u32[]{:S(2)}) copy-start(s32[1,32,1]{1,2,0:T(1,128)} %param.13) | copy-start | bytes 388
  0.7 26.6 %copy-start.14 = (f32[1,128]{1,0:T(1,128)S(1)}, f32[1,128]{1,0:T(1,128)}, u32[]{:S(2)}) copy-start(f32[1,128]{1,0:T(1,128)} %param.11) | copy-start | bytes 1540
  0.7 27.1 %copy-start.15 = (f32[1,32,128]{2,1,0:T(8,128)S(1)}, f32[1,32,128]{2,1,0:T(8,128)}, u32[]{:S(2)}) copy-start(f32[1,32,128]{2,1,0:T(8,128)} %param.15) | copy-start | bytes 49156
  0.7 27.1 %copy-start.18 = (s32[1,32]{1,0:T(1,128)S(1)}, s32[1,32]{1,0:T(1,128)}, u32[]{:S(2)}) copy-start(s32[1,32]{1,0:T(1,128)} %param.14) | copy-start | bytes 388
  9.1 18.0 %all-to-all-start = ((f32[32,2,2,4,128]{4,3,2,1,0:T(4,128)}), f32[32,2,2,4,128]{4,3,2,1,0:T(4,128)S(1)}, u32[]{:S(2)}, u32[]{:S(2)}) async-start(f32[32,2,2,4,128]{4,3,2,1,0:T(4,128)} %copy.81), calls=%async_computation | async-start | bytes 524288 | tf_op jit(solution)/shard_map/all_to_all | solution.py:104
  19.2 43.4 %collective-permute-start = (f32[3,2,128,128]{3,2,1,0:T(8,128)}, f32[3,2,128,128]{3,2,1,0:T(8,128)S(1)}, u32[]{:S(2)}, u32[]{:S(2)}) collective-permute-start(f32[3,2,128,128]{3,2,1,0:T(8,128)} %get-tuple-element.37), channel_id=1, source_target_pairs={{0,4},{4,8},{8,12},{12,16},{16,20},{20,24},{24,28},{28,32},{32,36}... | collective-permute-start | bytes 1179656 | tf_op jit(solution)/shard_map/ppermute | solution.py:19
  21.3 45.1 %collective-permute-start.1 = (f32[3,2,128,128]{3,2,1,0:T(8,128)}, f32[3,2,128,128]{3,2,1,0:T(8,128)S(1)}, u32[]{:S(2)}, u32[]{:S(2)}) collective-permute-start(f32[3,2,128,128]{3,2,1,0:T(8,128)} %get-tuple-element.36), channel_id=1, source_target_pairs={{4,0},{8,4},{12,8},{16,12},{20,16},{24,20},{28,24},{32,28},{36,32}... | collective-permute-start | bytes 1179656 | tf_op jit(solution)/shard_map/ppermute | solution.py:22
  28.6 17.0 %all-to-all-start.1 = ((f32[32,2,128]{2,1,0:T(2,128)}), f32[32,2,128]{2,1,0:T(2,128)S(1)}, u32[]{:S(2)}, u32[]{:S(2)}) async-start(f32[32,2,128]{2,1,0:T(2,128)} %copy.84), calls=%async_computation.1 | async-start | bytes 65536 | tf_op jit(solution)/shard_map/all_to_all | solution.py:113
  56.1 36.1 %collective-permute-start.3 = (f32[4,2,128,128]{3,2,1,0:T(8,128)}, f32[4,2,128,128]{3,2,1,0:T(8,128)S(1)}, u32[]{:S(2)}, u32[]{:S(2)}) collective-permute-start(f32[4,2,128,128]{3,2,1,0:T(8,128)} %get-tuple-element.33), channel_id=1, source_target_pairs={{4,0},{8,4},{12,8},{16,12},{20,16},{24,20},{28,24},{32,28},{36,32}... | collective-permute-start | bytes 1572872 | tf_op jit(solution)/shard_map/ppermute | solution.py:22
  60.7 31.5 %collective-permute-start.2 = (f32[4,2,128,128]{3,2,1,0:T(8,128)}, f32[4,2,128,128]{3,2,1,0:T(8,128)}, u32[]{:S(2)}, u32[]{:S(2)}) collective-permute-start(f32[4,2,128,128]{3,2,1,0:T(8,128)} %get-tuple-element.32), channel_id=1, source_target_pairs={{0,4},{4,8},{8,12},{12,16},{16,20},{20,24},{24,28},{28,32},{32,36}... | collective-permute-start | bytes 1572872 | tf_op jit(solution)/shard_map/ppermute | solution.py:19
  66.5 8.1 %collective-permute-start.5 = (f32[3,36,2,128]{3,2,1,0:T(2,128)S(1)}, f32[3,36,2,128]{3,2,1,0:T(2,128)S(1)}, u32[]{:S(2)}, u32[]{:S(2)}) collective-permute-start(f32[3,36,2,128]{3,2,1,0:T(2,128)S(1)} %get-tuple-element.35), channel_id=1, source_target_pairs={{1,0},{2,1},{3,2},{5,4},{6,5},{7,6},{9,8},{10,9},{11,10},{13,12},{... | collective-permute-start | bytes 331784 | tf_op jit(solution)/shard_map/ppermute | solution.py:22
  67.8 6.9 %collective-permute-start.4 = (f32[3,36,2,128]{3,2,1,0:T(2,128)S(1)}, f32[3,36,2,128]{3,2,1,0:T(2,128)S(1)}, u32[]{:S(2)}, u32[]{:S(2)}) collective-permute-start(f32[3,36,2,128]{3,2,1,0:T(2,128)S(1)} %get-tuple-element.34), channel_id=1, source_target_pairs={{0,1},{1,2},{2,3},{4,5},{5,6},{6,7},{8,9},{9,10},{10,11},{12,13},{... | collective-permute-start | bytes 331784 | tf_op jit(solution)/shard_map/ppermute | solution.py:19
  93.2 35.1 %collective-permute-start.7 = (f32[4,36,2,128]{3,1,2,0:T(8,128)S(1)}, f32[4,36,2,128]{3,1,2,0:T(8,128)S(1)}, u32[]{:S(2)}, u32[]{:S(2)}) collective-permute-start(f32[4,36,2,128]{3,1,2,0:T(8,128)S(1)} %copy.88), channel_id=1, source_target_pairs={{1,0},{2,1},{3,2},{5,4},{6,5},{7,6},{9,8},{10,9},{11,10},{13,12},{... | collective-permute-start | bytes 442376 | tf_op jit(solution)/shard_map/ppermute | solution.py:22
  94.5 33.8 %collective-permute-start.6 = (f32[4,36,2,128]{3,1,2,0:T(8,128)S(1)}, f32[4,36,2,128]{3,1,2,0:T(8,128)}, u32[]{:S(2)}, u32[]{:S(2)}) collective-permute-start(f32[4,36,2,128]{3,1,2,0:T(8,128)S(1)} %copy.86), channel_id=1, source_target_pairs={{0,1},{1,2},{2,3},{4,5},{5,6},{6,7},{8,9},{9,10},{10,11},{12,13},{... | collective-permute-start | bytes 442376 | tf_op jit(solution)/shard_map/ppermute | solution.py:19
  212.8 19.3 %copy-start.3 = (f32[1,32,128,128]{3,2,1,0:T(8,128)S(1)}, f32[1,32,128,128]{3,2,1,0:T(8,128)}, u32[]{:S(2)}) copy-start(f32[1,32,128,128]{3,2,1,0:T(8,128)} %copy-done.1) | copy-start | bytes 6291460
  252.1 35.2 %copy-start = (f32[4,32,128,128]{3,2,1,0:T(8,128)}, f32[4,32,128,128]{3,2,1,0:T(8,128)S(1)}, u32[]{:S(2)}) copy-start(f32[4,32,128,128]{3,2,1,0:T(8,128)S(1)} %fusion.12) | copy-start | bytes 25165828
  252.1 23.2 %copy-start.8 = (f32[1,33,128,128]{3,2,1,0:T(8,128)S(1)}, f32[1,33,128,128]{3,2,1,0:T(8,128)}, u32[]{:S(2)}) copy-start(f32[1,33,128,128]{3,2,1,0:T(8,128)} %get-tuple-element.17) | copy-start | bytes 6488068
  252.1 23.2 %copy-start.13 = (pred[33,128,128]{2,1,0:T(8,128)(4,1)S(1)}, pred[33,128,128]{2,1,0:T(8,128)(4,1)}, u32[]{:S(2)}) copy-start(pred[33,128,128]{2,1,0:T(8,128)(4,1)} %get-tuple-element.16) | copy-start | bytes 1622020
  252.2 11.1 %collective-permute-start.9 = (f32[4,2,128,128]{3,2,1,0:T(8,128)S(1)}, f32[4,2,128,128]{3,2,1,0:T(8,128)S(1)}, u32[]{:S(2)}, u32[]{:S(2)}) collective-permute-start(f32[4,2,128,128]{3,2,1,0:T(8,128)S(1)} %get-tuple-element.29), channel_id=1, source_target_pairs={{4,0},{8,4},{12,8},{16,12},{20,16},{24,20},{28,24},{32,28},{36,32}... | collective-permute-start | bytes 1572872 | tf_op jit(solution)/shard_map/ppermute | solution.py:22
  256.7 12.6 %collective-permute-start.8 = (f32[4,2,128,128]{3,2,1,0:T(8,128)S(1)}, f32[4,2,128,128]{3,2,1,0:T(8,128)S(1)}, u32[]{:S(2)}, u32[]{:S(2)}) collective-permute-start(f32[4,2,128,128]{3,2,1,0:T(8,128)S(1)} %get-tuple-element.28), channel_id=1, source_target_pairs={{0,4},{4,8},{8,12},{12,16},{16,20},{20,24},{24,28},{28,32},{32,36}... | collective-permute-start | bytes 1572872 | tf_op jit(solution)/shard_map/ppermute | solution.py:19
  269.3 18.1 %copy-start.9 = (f32[4,2,128,128]{3,2,1,0:T(8,128)}, f32[4,2,128,128]{3,2,1,0:T(8,128)S(1)}, u32[]{:S(2)}) copy-start(f32[4,2,128,128]{3,2,1,0:T(8,128)S(1)} %collective-permute-done.8) | copy-start | bytes 1572868
  269.4 17.8 %collective-permute-start.11 = (f32[4,36,2,128]{3,1,2,0:T(8,128)S(1)}, f32[4,36,2,128]{3,1,2,0:T(8,128)S(1)}, u32[]{:S(2)}, u32[]{:S(2)}) collective-permute-start(f32[4,36,2,128]{3,1,2,0:T(8,128)S(1)} %copy.94), channel_id=1, source_target_pairs={{1,0},{2,1},{3,2},{5,4},{6,5},{7,6},{9,8},{10,9},{11,10},{13,12},{... | collective-permute-start | bytes 442376 | tf_op jit(solution)/shard_map/ppermute | solution.py:22
  270.7 16.5 %collective-permute-start.10 = (f32[4,36,2,128]{3,1,2,0:T(8,128)S(1)}, f32[4,36,2,128]{3,1,2,0:T(8,128)S(1)}, u32[]{:S(2)}, u32[]{:S(2)}) collective-permute-start(f32[4,36,2,128]{3,1,2,0:T(8,128)S(1)} %copy.92), channel_id=1, source_target_pairs={{0,1},{1,2},{2,3},{4,5},{5,6},{6,7},{8,9},{9,10},{10,11},{12,13},{... | collective-permute-start | bytes 442376 | tf_op jit(solution)/shard_map/ppermute | solution.py:19
  343.0 28.9 %slice-start = ((s8[8388608]{0:T(1024)(128)(4,1)}), s8[4194304]{0:T(1024)(128)(4,1)S(1)}, s32[]{:S(2)}) async-start(s8[8388608]{0:T(1024)(128)(4,1)} %bitcast.60), calls=%async_computation.2 | async-start | bytes 8388608
  (16 other events, 192.4 us)
where the time goes:
time: 401 us; the launch traced here: 396 us
  other arithmetic  294 us (73%)
  starting transfers between devices  53.1 us (13%)
  local copies, waits for them, and re-layouts  35.1 us (9%)
  waiting for transfers between devices  10.8 us (3%)
    select_n x6, other arithmetic, divergence(): fluxes = jnp.where(face_speed > 0, upwind, downwind)  154 us
    concatenate x6, other arithmetic, extended(): block = jnp.concatenate([low, block, high], axis=dim)  79.6 us
    sub x2, other arithmetic, advance(): return inner - time_step * (along_x + along_y + along_z)  43.2 us
    ppermute x6, starting transfers between devices, extended(): lax.ppermute(lax.slice_in_dim(block, block.shape[dim] - width, None, axis...  21.2 us
    ppermute x6, starting transfers between devices, extended(): lax.ppermute(lax.slice_in_dim(block, 0, width, axis=dim), axis, backward)  18.5 us
    unnamed x55, local copies, waits for them, and re-layouts  8.89 us
    broadcast_in_dim x3, other arithmetic, divergence(): fluxes = jnp.where(face_speed > 0, upwind, downwind)  8.78 us
    all_to_all x1, starting transfers between devices, shards(): lax.all_to_all(packed, 'gx', split_axis=0, concat_axis=0, tiled=True)  8.05 us
  transfers between devices with their start and end apart: 14, of which 2 were waited for; matrix products, arithmetic and copies ran while one was open for 22% of the time, Pallas kernels for 0%

commit v1 on v0

v1 whole, which is shorter than its diff:
```python
import functools

import jax
import jax.numpy as jnp
from jax import lax
from jax.experimental import pallas as pl
from jax.experimental.pallas import tpu as pltpu
from jax.sharding import PartitionSpec as P

MESH = pl.DeviceIdType.MESH
f32 = jnp.float32
profile_weights = (0.4, 0.3, 0.2, 0.1)
SCALE = 0.1 * 0.25
X = 32
PAIRS = X // 2
ROWS = 144
OWN = pl.ds(8, 128)
N = 17
GX, GY = 32, 4


def S(k):
    return pl.ds(4 + k, 8, stride=N)


def A(k):
    return pl.ds(8 * k, 8)


def minmod(a, b):
    return jnp.maximum(jnp.minimum(a, b), jnp.minimum(jnp.maximum(a, b), 0.0))


def rollup(v):
    return pltpu.roll(v, 7, 0)


def rolldn(v):
    return pltpu.roll(v, 1, 0)


class Line:
    def __init__(self, load):
        self.load = load
        v0, v15, v16 = load(0), load(15), load(16)
        wrap = rollup(v0) - v16
        before = v16 - v15
        twice = v16 + v16
        m = minmod(wrap, before)
        self.tail = (twice + m, twice - m, before)
        self.v = v0
        self.d = rolldn(wrap)
        self.l = rolldn(twice + m)
        self.f = None

    def step(self, k, w, mask):
        if k == 16:
            l, r, d = self.tail
        else:
            v = self.v
            ahead = self.load(k + 1)
            d = ahead - v if k < 15 else self.tail[2]
            if k % 2 == 0:
                self.clip = jnp.maximum(d, 0.0), jnp.minimum(d, 0.0)
                m = jnp.maximum(jnp.minimum(self.d, self.clip[0]), self.clip[1])
            else:
                m = jnp.maximum(jnp.minimum(d, self.clip[0]), self.clip[1])
            twice = v + v
            l, r = twice + m, twice - m
            self.v = ahead
        f = w * jnp.where(mask, self.l, r)
        out = None if self.f is None else f - self.f
        if k == 0:
            self.first = rollup(f)
        self.f, self.l, self.d = f, l, d
        return out

    def end(self):
        return self.first - self.f


def turn_in(i, c, b, q, qt):
    qt[2 * c + b, OWN, :] = q[c, i + 2 + b, OWN, :].T


def turn_out(c, b, zt, az):
    az[2 * c + b, OWN, :] = zt[2 * c + b, OWN, :].T


def zplane(i, b, comps, qt, zt, wz):
    lines = {c: Line(lambda k, c=c: qt[2 * c + b, S(k), :]) for c in comps}
    for k in range(N):
        w = wz[i + b, A(k), :]
        mask = w > 0
        for c in comps:
            out = lines[c].step(k, w, mask)
            if k:
                zt[2 * c + b, S(k - 1), :] = out
    for c in comps:
        zt[2 * c + b, S(16), :] = lines[c].end()


def xypair(i, comps, q, write, wx, wy, az, cx):
    lines = {
        (c, b): Line(lambda k, c=c, b=b: q[c, i + 2 + b, S(k), :]) for c in comps for b in range(2)
    }
    for k in range(N + 1):
        acc = {}
        if k < N:
            for b in range(2):
                w = wy[i + b, A(k), :]
                mask = w > 0
                for c in comps:
                    acc[c, b] = lines[c, b].step(k, w, mask)
        else:
            for key, line in lines.items():
                acc[key] = line.end()
        if k == 0:
            continue
        u = k - 1
        w0 = wx[i + 1, A(u), :]
        w1 = wx[i + 2, A(u), :]
        m0, m1 = w0 > 0, w1 > 0
        for c in comps:
            q1 = q[c, i + 3, S(u), :]
            q2 = q[c, i + 4, S(u), :]
            db = q2 - q1
            dc = q[c, i + 5, S(u), :] - q2
            high, low = jnp.maximum(db, 0.0), jnp.minimum(db, 0.0)
            s1 = jnp.maximum(jnp.minimum(cx[c, 0, A(u), :], high), low)
            s2 = jnp.maximum(jnp.minimum(dc, high), low)
            t1 = q1 + q1
            t2 = q2 + q2
            f0 = w0 * jnp.where(m0, cx[c, 1, A(u), :], t1 - s1)
            f1 = w1 * jnp.where(m1, t1 + s1, t2 - s2)
            fm = cx[c, 2, A(u), :]
            cx[c, 0, A(u), :] = dc
            cx[c, 1, A(u), :] = t2 + s2
            cx[c, 2, A(u), :] = f1
            write(c, i, u, q[c, i + 2, S(u), :] - ((f0 - fm) + (acc[c, 0] + az[2 * c, S(u), :])))
            write(c, i + 1, u, q1 - ((f1 - f0) + (acc[c, 1] + az[2 * c + 1, S(u), :])))


def xstart(comps, q, wx, cx):
    for u in range(N):
        w = wx[0, A(u), :]
        mask = w > 0
        for c in comps:
            qa, qb, qc, qd = (q[c, p, S(u), :] for p in range(4))
            db, dc = qc - qb, qd - qc
            left = (qb + qb) + minmod(qb - qa, db)
            m = minmod(db, dc)
            twice = qc + qc
            cx[c, 0, A(u), :] = dc
            cx[c, 1, A(u), :] = twice + m
            cx[c, 2, A(u), :] = w * jnp.where(mask, left, twice - m)


def zstart(groups, q, qt, zt, wz):
    for comps in groups:
        for b in range(2):
            for c in comps:
                turn_in(0, c, b, q, qt)
    for comps in groups:
        for b in range(2):
            zplane(0, b, comps, qt, zt, wz)
            for c in comps:
                turn_in(2, c, b, q, qt)


def sweep_step(j, groups, q, write, wx, wy, wz, cx, qt, zt, az):
    i = 2 * j
    nxt = jnp.minimum(i + 2, X - 2)
    nxt2 = jnp.minimum(i + 4, X - 2)
    for comps in groups:
        for b in range(2):
            for c in comps:
                turn_out(c, b, zt, az)
    for comps in groups:
        for b in range(2):
            zplane(nxt, b, comps, qt, zt, wz)
            for c in comps:
                turn_in(nxt2, c, b, q, qt)
    for comps in groups:
        xypair(i, comps, q, write, wx, wy, az, cx)


def clear_turned(qt):
    zero = jnp.zeros((8, 128), f32)
    for s in range(8):
        qt[s, 0:8, :] = zero
        qt[s, 136:144, :] = zero


def first_kernel(
    state, vel, thr, tile, parcel, count, share,
    q1, wxo, wyo, wzo, flux_out,
    q, v, q1v, wx, wy, wz, cx, qt, zt, az, stress, packed, got, rows, landed, zeros, zrows,
    load_sem, lsend, lrecv, a2a_sem, out_sem,
):
    gx, gy = lax.axis_index("gx"), lax.axis_index("gy")

    def local(src, dst, s):
        return pltpu.make_async_copy(src, dst, load_sem.at[s])

    loads = [
        local(vel.at[a], v.at[a, pl.ds(1, X), OWN, :], a) for a in range(3)
    ] + [local(state.at[c], q.at[c, pl.ds(2, X), OWN, :], 3 + c) for c in range(4)]
    for copy in loads:
        copy.start()

    target = (gx < GX - 1, gx > 0, gy < GY - 1, gy > 0)
    source = (gx > 0, gx < GX - 1, gy > 0, gy < GY - 1)
    where = (
        {"gx": lax.rem(gx + 1, GX)},
        {"gx": lax.rem(gx + GX - 1, GX)},
        {"gy": lax.rem(gy + 1, GY)},
        {"gy": lax.rem(gy + GY - 1, GY)},
    )

    class Exchange:
        def __init__(self, g, pieces):
            self.copies = [
                pltpu.make_async_remote_copy(
                    src_ref=src, dst_ref=dst, send_sem=lsend.at[g, n], recv_sem=lrecv.at[g, n],
                    device_id=where[n], device_id_type=MESH,
                )
                for n, (src, dst) in enumerate(pieces)
            ]

        def each(self, flags, act):
            for flag, copy in zip(flags, self.copies):
                @pl.when(flag)
                def _(copy=copy):
                    act(copy)

        def start(self):
            self.each(target, lambda copy: copy.start())

        def wait_recv(self):
            self.each(source, lambda copy: copy.wait_recv())

        def wait_send(self):
            self.each(target, lambda copy: copy.wait_send())

    all_x = pl.ds(2, X)
    wind = Exchange(0, [
        (vel.at[0, X - 1], v.at[0, 0, OWN, :]),
        (vel.at[0, 0], v.at[0, X + 1, OWN, :]),
        (vel.at[1, :, pl.ds(127, 1), :], v.at[1, pl.ds(1, X), pl.ds(7, 1), :]),
        (vel.at[1, :, pl.ds(0, 1), :], v.at[1, pl.ds(1, X), pl.ds(136, 1), :]),
    ])
    three = pl.ds(0, 3)
    spin = Exchange(1, [
        (state.at[three, pl.ds(X - 2, 2)], q.at[three, pl.ds(0, 2), OWN, :]),
        (state.at[three, pl.ds(0, 2)], q.at[three, pl.ds(X + 2, 2), OWN, :]),
        (state.at[three, :, pl.ds(126, 2), :], q.at[three, all_x, pl.ds(6, 2), :]),
        (state.at[three, :, pl.ds(0, 2), :], q.at[three, all_x, pl.ds(136, 2), :]),
    ])
    dust = Exchange(2, [
        (q.at[3, pl.ds(X, 2), OWN, :], q.at[3, pl.ds(0, 2), OWN, :]),
        (q.at[3, pl.ds(2, 2), OWN, :], q.at[3, pl.ds(X + 2, 2), OWN, :]),
        (q.at[3, all_x, pl.ds(134, 2), :], q.at[3, all_x, pl.ds(6, 2), :]),
        (q.at[3, all_x, pl.ds(8, 2), :], q.at[3, all_x, pl.ds(136, 2), :]),
    ])

    def later(g, cs):
        return Exchange(g, [
            (q1v.at[cs, pl.ds(X - 2, 2), OWN, :], q1.at[cs, pl.ds(0, 2), OWN, :]),
            (q1v.at[cs, pl.ds(0, 2), OWN, :], q1.at[cs, pl.ds(X + 2, 2), OWN, :]),
            (q1v.at[cs, :, pl.ds(134, 2), :], q1.at[cs, all_x, pl.ds(6, 2), :]),
            (q1v.at[cs, :, pl.ds(8, 2), :], q1.at[cs, all_x, pl.ds(136, 2), :]),
        ])

    spin1 = later(3, three)
    dust1 = later(4, pl.ds(3, 1))

    barrier = pltpu.get_barrier_semaphore()

    def peer(j):
        return lax.rem(gx + j, GX)

    def greet(j, _):
        pl.semaphore_signal(barrier, inc=1, device_id={"gx": peer(j)}, device_id_type=MESH)
        return 0

    lax.fori_loop(1, GX, greet, 0)
    for n in (2, 3):
        @pl.when(target[n])
        def _(n=n):
            pl.semaphore_signal(barrier, inc=1, device_id=where[n], device_id_type=MESH)
    pl.semaphore_wait(
        barrier, GX - 1 + source[2].astype(jnp.int32) + source[3].astype(jnp.int32))

    wind.start()
    spin.start()

    clear_turned(qt)
    zero_plane = jnp.zeros((128, 128), f32)
    zeros[...] = jnp.zeros(zeros.shape, f32)
    zrows[...] = jnp.zeros(zrows.shape, f32)

    @pl.when(gx == 0)
    def _():
        v[0, 0, OWN, :] = zero_plane
        for c in range(4):
            for p in range(2):
                q[c, p, OWN, :] = zero_plane

    @pl.when(gx == GX - 1)
    def _():
        v[0, X + 1, OWN, :] = zero_plane
        for c in range(4):
            for p in range(2):
                q[c, X + 2 + p, OWN, :] = zero_plane

    def clear_rows(lo, vrow):
        def body(x, _):
            v[1, x + 1, pl.ds(vrow, 1), :] = jnp.zeros((1, 128), f32)
            for c in range(4):
                q[c, x + 2, pl.ds(lo, 2), :] = jnp.zeros((2, 128), f32)
            return 0
        lax.fori_loop(0, X, body, 0)

    @pl.when(gy == 0)
    def _():
        clear_rows(6, 7)

    @pl.when(gy == GY - 1)
    def _():
        clear_rows(136, 136)

    def edge(src, dst, n):
        return pltpu.make_async_copy(src, dst, out_sem.at[n])

    edges = [
        (gx == 0, edge(zeros, q1.at[:, pl.ds(0, 2), OWN, :], 0)),
        (gx == GX - 1, edge(zeros, q1.at[:, pl.ds(X + 2, 2), OWN, :], 1)),
        (gy == 0, edge(zrows, q1.at[:, all_x, pl.ds(6, 2), :], 2)),
        (gy == GY - 1, edge(zrows, q1.at[:, all_x, pl.ds(136, 2), :], 3)),
    ]
    for flag, copy in edges:
        pl.when(flag)(copy.start)

    loads[0].wait()
    loads[1].wait()

    def friction(g, _):
        for h in range(8):
            x = g * 8 + h
            east, north = v[0, x + 1, OWN, :], v[1, x + 1, OWN, :]
            levels = (east * east + north * north).T
            total = profile_weights[0] * levels[0:1]
            for level in range(1, 4):
                total = total + profile_weights[level] * levels[level:level + 1]
            stress[pl.ds(x, 1), :] = total
        return 0

    lax.fori_loop(0, X // 8, friction, 0)

    def column(row):
        spot = lax.broadcasted_iota(jnp.int32, (X, X), 0) == lax.broadcasted_iota(jnp.int32, (X, X), 1)
        return jnp.sum(jnp.where(spot, jnp.broadcast_to(row, (X, X)), 0.0), axis=1, keepdims=True)

    highest = lax.Precision.HIGHEST
    owner = tile[...].astype(f32)
    same = jnp.broadcast_to(owner, (X, X)) == column(owner)
    sooner = lax.broadcasted_iota(jnp.int32, (X, X), 0) < lax.broadcasted_iota(jnp.int32, (X, X), 1)
    rank = jnp.sum(jnp.where(same & sooner, 1.0, 0.0), axis=0, keepdims=True)
    slot = owner * 2.0 + rank
    placing = jnp.where(
        jnp.broadcast_to(slot, (2 * GX, X))
        == lax.broadcasted_iota(jnp.int32, (2 * GX, X), 0).astype(f32), 1.0, 0.0)
    packed[...] = jnp.dot(placing, stress[...], precision=highest, preferred_element_type=f32)

    def tiles_to(j):
        o = peer(j)
        return pltpu.make_async_remote_copy(
            src_ref=packed.at[pl.ds(2 * o, 2), :], dst_ref=got.at[pl.ds(2 * gx, 2), :],
            send_sem=a2a_sem.at[0], recv_sem=a2a_sem.at[1],
            device_id={"gx": o}, device_id_type=MESH)

    def rows_to(j):
        o = peer(j)
        return pltpu.make_async_remote_copy(
            src_ref=rows.at[pl.ds(o, 1), :], dst_ref=landed.at[pl.ds(gx, 1), :],
            send_sem=a2a_sem.at[2], recv_sem=a2a_sem.at[3],
            device_id={"gx": o}, device_id_type=MESH)

    def send_all(copy):
        def body(j, _):
            copy(j).start()
            return 0
        lax.fori_loop(1, GX, body, 0)

    def wait_all(ref, count, s):
        part = ref.at[pl.ds(0, count), :]
        pltpu.make_async_copy(part, part, a2a_sem.at[s]).wait()

    send_all(tiles_to)
    got[pl.ds(2 * gx, 2), :] = packed[pl.ds(2 * gx, 2), :]

    loads[2].wait()
    wind.wait_recv()

    def speeds(i, b):
        for k in range(N):
            wx[i, A(k), :] = SCALE * (v[0, i, S(k), :] + v[0, i + 1, S(k), :])
            wy[i, A(k), :] = SCALE * (v[1, i + 1, pl.ds(3 + k, 8, stride=N), :] + v[1, i + 1, S(k), :])
            wz[i, A(k), :] = SCALE * (qt[b, pl.ds(3 + k, 8, stride=N), :] + qt[b, S(k), :])

    def make_speeds(g, _):
        for b in range(8):
            qt[b, OWN, :] = v[2, g * 8 + b + 1, OWN, :].T
        for b in range(8):
            speeds(g * 8 + b, b)
        return 0

    lax.fori_loop(0, X // 8, make_speeds, 0)
    for k in range(N):
        wx[X, A(k), :] = SCALE * (v[0, X, S(k), :] + v[0, X + 1, S(k), :])
    winds_out = [pltpu.make_async_copy(a, b, out_sem.at[4 + n])
                 for n, (a, b) in enumerate(((wx, wxo), (wy, wyo), (wz, wzo)))]
    for copy in winds_out:
        copy.start()

    def parcels():
        wait_all(got, 2 * (GX - 1), 1)
        lifting = jnp.maximum(got[...] - thr[...], 0.0)
        flux = jnp.sum(lifting, axis=0, keepdims=True) / X
        flux_out[...] = flux
        reach = lax.broadcasted_iota(jnp.int32, (X, 128), 1).astype(f32) < column(count[...].astype(f32))
        masses = flux * share[...] * jnp.where(reach, 1.0, 0.0)
        going = jnp.where(
            jnp.broadcast_to(parcel[...], (GX, X)) == lax.broadcasted_iota(jnp.int32, (GX, X), 0), 1.0, 0.0)
        rows[...] = jnp.dot(going, masses, precision=highest, preferred_element_type=f32)
        send_all(rows_to)
        landed[pl.ds(gx, 1), :] = rows[pl.ds(gx, 1), :]

    def deposit():
        wait_all(landed, GX - 1, 3)
        loads[6].wait()
        top = lax.broadcasted_iota(jnp.int32, (128, 128), 0) == 0

        def body(g, _):
            for h in range(8):
                x = g * 8 + h
                drop = jnp.where(top, jnp.broadcast_to(landed[pl.ds(x, 1), :], (128, 128)), 0.0).T
                q[3, x + 2, OWN, :] = q[3, x + 2, OWN, :] + drop
            return 0

        lax.fori_loop(0, X // 8, body, 0)
        dust.start()

    def keep(c, x, u, value):
        q1v[c, x, S(u), :] = value

    def out_pair(comps, j):
        lo, hi = comps[0], comps[-1] + 1
        return pltpu.make_async_copy(
            q1v.at[pl.ds(lo, hi - lo), pl.ds(2 * j, 2), OWN, :],
            q1.at[pl.ds(lo, hi - lo), pl.ds(2 * j + 2, 2), OWN, :], out_sem.at[7 + lo])

    def sweep(groups, comps, extra):
        xstart(comps, q, wx, cx)
        zstart(groups, q, qt, zt, wz)

        def body(j, _):
            extra(j)
            sweep_step(j, groups, q, keep, wx, wy, wz, cx, qt, zt, az)
            out_pair(comps, j).start()
            return 0

        lax.fori_loop(0, PAIRS, body, 0)

    for c in range(3):
        loads[3 + c].wait()
    spin.wait_recv()

    def extra(j):
        pl.when(j == 4)(parcels)
        pl.when(j == 9)(deposit)

    clear_turned(qt)
    sweep(((0, 1, 2),), (0, 1, 2), extra)
    spin1.start()
    dust.wait_recv()
    sweep(((3,),), (3,), lambda j: None)
    dust1.start()

    for comps in ((0, 1, 2), (3,)):
        lo, hi = comps[0], comps[-1] + 1
        pltpu.make_async_copy(
            q1v.at[pl.ds(lo, hi - lo), :, OWN, :],
            q1.at[pl.ds(lo, hi - lo), all_x, OWN, :], out_sem.at[7 + lo]).wait()
    for copy in winds_out:
        copy.wait()
    for flag, copy in edges:
        pl.when(flag)(copy.wait)
    wait_all(packed, 2 * (GX - 1), 0)
    wait_all(rows, GX - 1, 2)
    wind.wait_send()
    spin.wait_send()
    dust.wait_send()
    spin1.wait_send()
    dust1.wait_send()
    spin1.wait_recv()
    dust1.wait_recv()


def second_kernel(q1, wxi, wyi, wzi, flux_in, out, flux_out, q, wx, wy, wz, ov, cx, qt, zt, az, sem, osem):
    def q_copy(j):
        return pltpu.make_async_copy(q1.at[:, pl.ds(2 * j, 2)], q.at[:, pl.ds(2 * j, 2)], sem.at[0, j])

    def w_copies(j):
        k = pl.ds(2 * j, 2)
        return [pltpu.make_async_copy(a.at[k], b.at[k], sem.at[1 + n, j])
                for n, (a, b) in enumerate(((wxi, wx), (wyi, wy), (wzi, wz)))]

    last = pltpu.make_async_copy(wxi.at[pl.ds(X, 1)], wx.at[pl.ds(X, 1)], sem.at[1, PAIRS])

    def begin(j, _):
        q_copy(j).start()
        for copy in w_copies(j):
            copy.start()
        return 0

    lax.fori_loop(0, PAIRS, begin, 0)
    q_copy(PAIRS).start()
    q_copy(PAIRS + 1).start()
    last.start()
    flux_out[...] = flux_in[...]
    clear_turned(qt)
    groups = ((0, 1), (2, 3))
    comps = (0, 1, 2, 3)
    for j in range(3):
        q_copy(j).wait()
    for copy in w_copies(0):
        copy.wait()

    def keep(c, x, u, value):
        ov[c, x, S(u), :] = value

    def out_pair(j):
        return pltpu.make_async_copy(
            ov.at[:, pl.ds(2 * j, 2), OWN, :], out.at[:, pl.ds(2 * j, 2)], osem.at[0])

    xstart(comps, q, wx, cx)
    zstart(groups, q, qt, zt, wz)

    def body(j, _):
        @pl.when(j < PAIRS - 1)
        def _():
            q_copy(j + 3).wait()
            for copy in w_copies(j + 1):
                copy.wait()

        @pl.when(j == PAIRS - 1)
        def _():
            last.wait()

        sweep_step(j, groups, q, keep, wx, wy, wz, cx, qt, zt, az)
        out_pair(j).start()
        return 0

    lax.fori_loop(0, PAIRS, body, 0)
    pltpu.make_async_copy(ov.at[:, :, OWN, :], out, osem.at[0]).wait()


def shards(state, velocity, threshold, tile_owner, parcel_owner, parcel_count, parcel_share):
    def vm(*shape):
        return pltpu.VMEM(shape, f32)

    def like(*shape):
        return jax.ShapeDtypeStruct(shape, f32)

    hbm = pl.BlockSpec(memory_space=pl.ANY)
    vmem = pl.BlockSpec(memory_space=pltpu.VMEM)
    work = [vm(4, 3, 8 * N, 128)] + [vm(8, ROWS, 128)] * 3
    speeds = [vm(X + 1, 8 * N, 128), vm(X, 8 * N, 128), vm(X, 8 * N, 128)]
    q1, wx, wy, wz, flux = pl.pallas_call(
        first_kernel,
        out_shape=(like(4, X + 4, ROWS, 128), like(X + 1, 8 * N, 128), like(X, 8 * N, 128),
                   like(X, 8 * N, 128), like(1, 128)),
        in_specs=[hbm, hbm] + [vmem] * 5,
        out_specs=(hbm, hbm, hbm, hbm, vmem),
        scratch_shapes=[vm(4, X + 4, ROWS, 128), vm(3, X + 2, ROWS, 128), vm(4, X, ROWS, 128)]
        + speeds + work
        + [vm(X, 128), vm(2 * GX, 128), vm(2 * GX, 128), vm(GX, 128), vm(GX, 128), vm(4, 2, 128, 128), vm(4, X, 2, 128),
           pltpu.SemaphoreType.DMA((7,)), pltpu.SemaphoreType.DMA((5, 4)), pltpu.SemaphoreType.DMA((5, 4)),
           pltpu.SemaphoreType.DMA((4,)), pltpu.SemaphoreType.DMA((11,))],
        compiler_params=pltpu.CompilerParams(
            collective_id=0, has_side_effects=True, vmem_limit_bytes=56 << 20),
    )(state, velocity, threshold, tile_owner.reshape(1, X), parcel_owner.reshape(1, X),
      parcel_count, parcel_share.reshape(X, 128))
    return pl.pallas_call(
        second_kernel,
        out_shape=(like(4, X, 128, 128), like(1, 128)),
        in_specs=[hbm] * 4 + [vmem],
        out_specs=(hbm, vmem),
        scratch_shapes=[vm(4, X + 4, ROWS, 128)] + speeds + [vm(4, X, ROWS, 128)] + work
        + [pltpu.SemaphoreType.DMA((4, PAIRS + 2)), pltpu.SemaphoreType.DMA((1,))],
        compiler_params=pltpu.CompilerParams(vmem_limit_bytes=56 << 20),
    )(q1, wx, wy, wz, flux)


def solution(mesh):
    return jax.shard_map(
        shards,
        mesh=mesh,
        in_specs=(
            P(None, "gx", "gy", None),
            P(None, "gx", "gy", None),
            P("gx", "gy"),
            P("gy", "gx", None),
            P("gy", "gx", None),
            P("gy", "gx"),
            P("gy", "gx", None),
        ),
        out_specs=(P(None, "gx", "gy", None), P("gx", "gy")),
        check_vma=False,
    )
```

time: 401 us -> 55.1 us (0.14)
  the two profiles are of different devices: /device:TPU:32 before, /device:TPU:1 now
where the time goes in v1:
time: 55.1 us; the launch traced here: 54.9 us
  Pallas kernels  54.3 us (99%)
  between operations  0.64 us (1%)
    pallas_call x1, Pallas kernels, shards(): pl.pallas_call(first_kernel, out_shape=(like(4, X + 4, ROWS, 128), like(X...  37.4 us
    pallas_call x1, Pallas kernels, shards(): pl.pallas_call(second_kernel, out_shape=(like(4, X, 128, 128), like(1, 12...  16.9 us

profile of v1, /device:TPU:1, one launch (start us, length us, event | category | flops | bytes accessed | tf_op | source)
XLA Modules:
  0.0 54.9 jit_solution(13729133474376864074)
XLA Ops:
  0.6 37.4 %shard_map.86 = (f32[4,36,144,128]{3,2,1,0:T(8,128)}, f32[33,136,128]{2,1,0:T(8,128)}, f32[32,136,128]{2,1,0:T(8,128)}, f32[32,136,128]{2,1,0:T(8,128)}, f32[1,128]{1,0:T(1,128)}) custom-call(f32[4,32,128,128]{3,2,1,0:T(8,128)} %state.1, f32[3,32,128,128]{3,2,1,0:T(8,128)} %vel.1, f32[1,128]{1,0:T(1,128)} %thr.1, s32[1,32]{1,0:T(1,128)} %bitcast.4, ...), custom_call_target="tpu_custom_call" | custom-call | tf_op jit(solution)/shard_map/pallas_call | solution.py:581
  38.0 16.9 %shard_map.87 = (f32[4,32,128,128]{3,2,1,0:T(8,128)}, f32[1,128]{1,0:T(1,128)}) custom-call(f32[4,36,144,128]{3,2,1,0:T(8,128)} %get-tuple-element.7.q1, f32[33,136,128]{2,1,0:T(8,128)} %get-tuple-element.8.wxi, f32[32,136,128]{2,1,0:T(8,128)} %get-tuple-element.9.wyi, f32[32,136,128]{2,1,0:T(8,128)} %get-tuple-element.10.wzi, ...), custom_call_target="tpu_custom_call" | custom-call | tf_op jit(solution)/shard_map/pallas_call | solution.py:596

commit v2 on v1

v2 whole, which is shorter than its diff:
```python
import jax
import jax.numpy as jnp
from jax import lax
from jax.experimental import pallas as pl
from jax.experimental.pallas import tpu as pltpu
from jax.sharding import PartitionSpec as P

MESH = pl.DeviceIdType.MESH
f32 = jnp.float32
profile_weights = (0.4, 0.3, 0.2, 0.1)
SCALE = 0.1 * 0.25
X = 32
PAIRS = X // 2
ROWS = 144
OWN = pl.ds(8, 128)
N = 17
GX, GY = 32, 4
PARCELS_AT, DEPOSIT_AT = 1, 6


def S(k):
    return pl.ds(4 + k, 8, stride=N)


def A(k):
    return pl.ds(8 * k, 8)


def minmod(a, b):
    return jnp.maximum(jnp.minimum(a, b), jnp.minimum(jnp.maximum(a, b), 0.0))


def rollup(v):
    return pltpu.roll(v, 7, 0)


def rolldn(v):
    return pltpu.roll(v, 1, 0)


class Line:
    def __init__(self, load):
        self.load = load
        v0, v15, v16 = load(0), load(15), load(16)
        wrap = rollup(v0) - v16
        before = v16 - v15
        twice = v16 + v16
        m = minmod(wrap, before)
        self.tail = (twice + m, twice - m, before)
        self.v = v0
        self.d = rolldn(wrap)
        self.l = rolldn(twice + m)
        self.f = None

    def step(self, k, w, mask):
        if k == 16:
            l, r, d = self.tail
        else:
            v = self.v
            ahead = self.load(k + 1)
            d = ahead - v if k < 15 else self.tail[2]
            if k % 2 == 0:
                self.clip = jnp.maximum(d, 0.0), jnp.minimum(d, 0.0)
                m = jnp.maximum(jnp.minimum(self.d, self.clip[0]), self.clip[1])
            else:
                m = jnp.maximum(jnp.minimum(d, self.clip[0]), self.clip[1])
            twice = v + v
            l, r = twice + m, twice - m
            self.v = ahead
        f = w * jnp.where(mask, self.l, r)
        out = None if self.f is None else f - self.f
        if k == 0:
            self.first = rollup(f)
        self.f, self.l, self.d = f, l, d
        return out

    def end(self):
        return self.first - self.f


def turn_in(i, c, b, q, qt):
    qt[2 * c + b, OWN, :] = q[c, i + 2 + b, OWN, :].T


def turn_out(c, b, zt, az):
    az[2 * c + b, OWN, :] = zt[2 * c + b, OWN, :].T


def zplane(i, b, comps, qt, zt, wz):
    lines = {c: Line(lambda k, c=c: qt[2 * c + b, S(k), :]) for c in comps}
    for k in range(N):
        w = wz[i + b, A(k), :]
        mask = w > 0
        for c in comps:
            out = lines[c].step(k, w, mask)
            if k:
                zt[2 * c + b, S(k - 1), :] = out
    for c in comps:
        zt[2 * c + b, S(16), :] = lines[c].end()


def xypair(i, comps, q, write, wx, wy, az, cx):
    lines = {
        (c, b): Line(lambda k, c=c, b=b: q[c, i + 2 + b, S(k), :]) for c in comps for b in range(2)
    }
    for k in range(N + 1):
        acc = {}
        if k < N:
            for b in range(2):
                w = wy[i + b, A(k), :]
                mask = w > 0
                for c in comps:
                    acc[c, b] = lines[c, b].step(k, w, mask)
        else:
            for key, line in lines.items():
                acc[key] = line.end()
        if k == 0:
            continue
        u = k - 1
        w0 = wx[i + 1, A(u), :]
        w1 = wx[i + 2, A(u), :]
        m0, m1 = w0 > 0, w1 > 0
        for c in comps:
            q1 = q[c, i + 3, S(u), :]
            q2 = q[c, i + 4, S(u), :]
            db = q2 - q1
            dc = q[c, i + 5, S(u), :] - q2
            high, low = jnp.maximum(db, 0.0), jnp.minimum(db, 0.0)
            s1 = jnp.maximum(jnp.minimum(cx[c, 0, A(u), :], high), low)
            s2 = jnp.maximum(jnp.minimum(dc, high), low)
            t1 = q1 + q1
            t2 = q2 + q2
            f0 = w0 * jnp.where(m0, cx[c, 1, A(u), :], t1 - s1)
            f1 = w1 * jnp.where(m1, t1 + s1, t2 - s2)
            fm = cx[c, 2, A(u), :]
            cx[c, 0, A(u), :] = dc
            cx[c, 1, A(u), :] = t2 + s2
            cx[c, 2, A(u), :] = f1
            write(c, i, u, q[c, i + 2, S(u), :] - ((f0 - fm) + (acc[c, 0] + az[2 * c, S(u), :])))
            write(c, i + 1, u, q1 - ((f1 - f0) + (acc[c, 1] + az[2 * c + 1, S(u), :])))


def xstart(i, comps, q, wx, cx):
    for u in range(N):
        w = wx[i, A(u), :]
        mask = w > 0
        for c in comps:
            qa, qb, qc, qd = (q[c, i + p, S(u), :] for p in range(4))
            db, dc = qc - qb, qd - qc
            left = (qb + qb) + minmod(qb - qa, db)
            m = minmod(db, dc)
            twice = qc + qc
            cx[c, 0, A(u), :] = dc
            cx[c, 1, A(u), :] = twice + m
            cx[c, 2, A(u), :] = w * jnp.where(mask, left, twice - m)


def sweep(groups, q, write, wx, wy, wz, cx, qt, zt, az, first, before, after):
    comps = [c for group in groups for c in group]

    def pair(j):
        return lax.rem(j + first, PAIRS)

    for group in groups:
        for b in range(2):
            for c in group:
                turn_in(2 * first, c, b, q, qt)
    for group in groups:
        for b in range(2):
            zplane(2 * first, b, group, qt, zt, wz)
            for c in group:
                turn_in(2 * first + 2, c, b, q, qt)
    xstart(2 * first, comps, q, wx, cx)

    def body(j, _):
        before(j)
        if first:
            pl.when(j == PAIRS - first)(lambda: xstart(0, comps, q, wx, cx))
        for group in groups:
            for b in range(2):
                for c in group:
                    turn_out(c, b, zt, az)
        for group in groups:
            for b in range(2):
                zplane(2 * pair(j + 1), b, group, qt, zt, wz)
                for c in group:
                    turn_in(2 * pair(j + 2), c, b, q, qt)
        for group in groups:
            xypair(2 * pair(j), group, q, write, wx, wy, az, cx)
        after(pair(j))
        return 0

    lax.fori_loop(0, PAIRS, body, 0)


def clear_turned(qt):
    zero = jnp.zeros((8, 128), f32)
    for s in range(8):
        qt[s, 0:8, :] = zero
        qt[s, 136:144, :] = zero


def first_kernel(
    state, vel, thr_in, tile_in, parcel_in, count_in, share_in,
    q1, wx, wy, wz, ov, flux_out,
    q, v, yh, cx, qt, zt, az, stress, packed, got, rows, landed, thr, tile, parcel, count, share,
    load_sem, lsend, lrecv, a2a_sem,
):
    gx, gy = lax.axis_index("gx"), lax.axis_index("gy")

    def local(src, dst, s):
        return pltpu.make_async_copy(src, dst, load_sem.at[s])

    loads = [
        local(vel.at[a], v.at[a, pl.ds(1, X), OWN, :], a) for a in range(3)
    ] + [local(state.at[c], q.at[c, pl.ds(2, X), OWN, :], 3 + c) for c in range(4)]
    loads[0].start()
    loads[1].start()
    small = [local(src, dst, 7 + n) for n, (src, dst) in enumerate(
        ((tile_in, tile), (thr_in, thr), (parcel_in, parcel), (count_in, count), (share_in, share)))]
    for copy in small:
        copy.start()

    target = (gx < GX - 1, gx > 0, gy < GY - 1, gy > 0)
    source = (gx > 0, gx < GX - 1, gy > 0, gy < GY - 1)
    where = (
        {"gx": lax.rem(gx + 1, GX)},
        {"gx": lax.rem(gx + GX - 1, GX)},
        {"gy": lax.rem(gy + 1, GY)},
        {"gy": lax.rem(gy + GY - 1, GY)},
    )
    along_x, along_y, both = (0, 1), (2, 3), (0, 1, 2, 3)

    class Exchange:
        def __init__(self, g, pieces):
            self.copies = [
                pltpu.make_async_remote_copy(
                    src_ref=src, dst_ref=dst, send_sem=lsend.at[g, n], recv_sem=lrecv.at[g, n],
                    device_id=where[n], device_id_type=MESH,
                )
                for n, (src, dst) in enumerate(pieces)
            ]

        def start(self, ways):
            for n in ways:
                pl.when(target[n])(self.copies[n].start)

        def wait_recv(self, ways):
            for n in ways:
                pl.when(source[n])(self.copies[n].wait_recv)

        def wait_send(self):
            for n in both:
                pl.when(target[n])(self.copies[n].wait_send)

    all_x = pl.ds(2, X)
    wind = Exchange(0, [
        (vel.at[0, X - 1], v.at[0, 0, OWN, :]),
        (vel.at[0, 0], v.at[0, X + 1, OWN, :]),
        (vel.at[1, :, pl.ds(127, 1), :], v.at[1, pl.ds(1, X), pl.ds(7, 1), :]),
        (vel.at[1, :, pl.ds(0, 1), :], v.at[1, pl.ds(1, X), pl.ds(136, 1), :]),
    ])
    three = pl.ds(0, 3)
    spin = Exchange(1, [
        (state.at[three, pl.ds(X - 2, 2)], q.at[three, pl.ds(0, 2), OWN, :]),
        (state.at[three, pl.ds(0, 2)], q.at[three, pl.ds(X + 2, 2), OWN, :]),
        (state.at[three, :, pl.ds(126, 2), :], q.at[three, all_x, pl.ds(6, 2), :]),
        (state.at[three, :, pl.ds(0, 2), :], q.at[three, all_x, pl.ds(136, 2), :]),
    ])
    dust = Exchange(2, [
        (q.at[3, pl.ds(X, 2), OWN, :], q.at[3, pl.ds(0, 2), OWN, :]),
        (q.at[3, pl.ds(2, 2), OWN, :], q.at[3, pl.ds(X + 2, 2), OWN, :]),
        (q.at[3, all_x, pl.ds(134, 2), :], q.at[3, all_x, pl.ds(6, 2), :]),
        (q.at[3, all_x, pl.ds(8, 2), :], q.at[3, all_x, pl.ds(136, 2), :]),
    ])
    second = [
        Exchange(3 + c, [
            (q1.at[c, pl.ds(X, 2), OWN, :], q1.at[c, pl.ds(0, 2), OWN, :]),
            (q1.at[c, pl.ds(2, 2), OWN, :], q1.at[c, pl.ds(X + 2, 2), OWN, :]),
            (q1.at[c, all_x, pl.ds(134, 2), :], yh.at[0, c]),
            (q1.at[c, all_x, pl.ds(8, 2), :], yh.at[1, c]),
        ])
        for c in range(4)
    ]

    barrier = pltpu.get_barrier_semaphore()

    def peer(j):
        return lax.rem(gx + j, GX)

    def greet(j, _):
        pl.semaphore_signal(barrier, inc=1, device_id={"gx": peer(j)}, device_id_type=MESH)
        return 0

    lax.fori_loop(1, GX, greet, 0)
    for n in along_y:
        @pl.when(target[n])
        def _(n=n):
            pl.semaphore_signal(barrier, inc=1, device_id=where[n], device_id_type=MESH)

    clear_turned(qt)
    zero_plane = jnp.zeros((128, 128), f32)

    def clear_planes(vp, p0):
        v[0, vp, OWN, :] = zero_plane
        for c in range(4):
            for p in range(2):
                q[c, p0 + p, OWN, :] = zero_plane
                q1[c, p0 + p, OWN, :] = zero_plane

    pl.when(gx == 0)(lambda: clear_planes(0, 0))
    pl.when(gx == GX - 1)(lambda: clear_planes(X + 1, X + 2))

    def clear_rows(side, lo, vrow):
        def body(x, _):
            v[1, x + 1, pl.ds(vrow, 1), :] = jnp.zeros((1, 128), f32)
            for c in range(4):
                q[c, x + 2, pl.ds(lo, 2), :] = jnp.zeros((2, 128), f32)
                yh[side, c, x] = jnp.zeros((2, 128), f32)
            return 0
        lax.fori_loop(0, X, body, 0)

    pl.when(gy == 0)(lambda: clear_rows(0, 6, 7))
    pl.when(gy == GY - 1)(lambda: clear_rows(1, 136, 136))

    loads[0].wait()
    loads[1].wait()
    for copy in loads[2:]:
        copy.start()

    def friction(g, _):
        for h in range(8):
            x = g * 8 + h
            east, north = v[0, x + 1, OWN, :], v[1, x + 1, OWN, :]
            levels = (east * east + north * north).T
            total = profile_weights[0] * levels[0:1]
            for level in range(1, 4):
                total = total + profile_weights[level] * levels[level:level + 1]
            stress[pl.ds(x, 1), :] = total
        return 0

    lax.fori_loop(0, X // 8, friction, 0)

    def column(row):
        spot = lax.broadcasted_iota(jnp.int32, (X, X), 0) == lax.broadcasted_iota(jnp.int32, (X, X), 1)
        return jnp.sum(jnp.where(spot, jnp.broadcast_to(row, (X, X)), 0.0), axis=1, keepdims=True)

    highest = lax.Precision.HIGHEST
    for copy in small:
        copy.wait()
    owner = tile[...].astype(f32)
    same = jnp.broadcast_to(owner, (X, X)) == column(owner)
    sooner = lax.broadcasted_iota(jnp.int32, (X, X), 0) < lax.broadcasted_iota(jnp.int32, (X, X), 1)
    rank = jnp.sum(jnp.where(same & sooner, 1.0, 0.0), axis=0, keepdims=True)
    slot = owner * 2.0 + rank
    placing = jnp.where(
        jnp.broadcast_to(slot, (2 * GX, X))
        == lax.broadcasted_iota(jnp.int32, (2 * GX, X), 0).astype(f32), 1.0, 0.0)
    packed[...] = jnp.dot(placing, stress[...], precision=highest, preferred_element_type=f32)

    def tiles_to(j):
        o = peer(j)
        return pltpu.make_async_remote_copy(
            src_ref=packed.at[pl.ds(2 * o, 2), :], dst_ref=got.at[pl.ds(2 * gx, 2), :],
            send_sem=a2a_sem.at[0], recv_sem=a2a_sem.at[1],
            device_id={"gx": o}, device_id_type=MESH)

    def rows_to(j):
        o = peer(j)
        return pltpu.make_async_remote_copy(
            src_ref=rows.at[pl.ds(o, 1), :], dst_ref=landed.at[pl.ds(gx, 1), :],
            send_sem=a2a_sem.at[2], recv_sem=a2a_sem.at[3],
            device_id={"gx": o}, device_id_type=MESH)

    def send_all(copy):
        def body(j, _):
            copy(j).start()
            return 0
        lax.fori_loop(1, GX, body, 0)

    def wait_all(ref, count, s):
        part = ref.at[pl.ds(0, count), :]
        pltpu.make_async_copy(part, part, a2a_sem.at[s]).wait()

    pl.semaphore_wait(
        barrier, GX - 1 + source[2].astype(jnp.int32) + source[3].astype(jnp.int32))
    send_all(tiles_to)
    wind.start(along_y)
    spin.start(along_y)
    spin.start(along_x)
    wind.start(along_x)
    got[pl.ds(2 * gx, 2), :] = packed[pl.ds(2 * gx, 2), :]

    def speed_x(i):
        for k in range(N):
            wx[i, A(k), :] = SCALE * (v[0, i, S(k), :] + v[0, i + 1, S(k), :])

    def speeds_x(i, _):
        speed_x(i)
        return 0

    lax.fori_loop(1, X, speeds_x, 0)
    loads[2].wait()

    def below(k):
        return pl.ds(3 + k, 8, stride=N)

    def speeds_z(g, _):
        for b in range(8):
            qt[b, OWN, :] = v[2, g * 8 + b + 1, OWN, :].T
        for b in range(8):
            for k in range(N):
                wz[g * 8 + b, A(k), :] = SCALE * (qt[b, below(k), :] + qt[b, S(k), :])
        return 0

    lax.fori_loop(0, X // 8, speeds_z, 0)
    wind.wait_recv(along_y)

    def speeds_y(i, _):
        for k in range(N):
            wy[i, A(k), :] = SCALE * (v[1, i + 1, below(k), :] + v[1, i + 1, S(k), :])
        return 0

    lax.fori_loop(0, X, speeds_y, 0)

    def parcels():
        wait_all(got, 2 * (GX - 1), 1)
        lifting = jnp.maximum(got[...] - thr[...], 0.0)
        flux = jnp.sum(lifting, axis=0, keepdims=True) / X
        flux_out[...] = flux
        reach = lax.broadcasted_iota(jnp.int32, (X, 128), 1).astype(f32) < column(count[...].astype(f32))
        masses = flux * share[...] * jnp.where(reach, 1.0, 0.0)
        going = jnp.where(
            jnp.broadcast_to(parcel[...], (GX, X)) == lax.broadcasted_iota(jnp.int32, (GX, X), 0), 1.0, 0.0)
        rows[...] = jnp.dot(going, masses, precision=highest, preferred_element_type=f32)
        send_all(rows_to)
        landed[pl.ds(gx, 1), :] = rows[pl.ds(gx, 1), :]

    def deposit():
        wait_all(landed, GX - 1, 3)
        loads[6].wait()
        top = lax.broadcasted_iota(jnp.int32, (128, 128), 0) == 0

        def body(g, _):
            for h in range(8):
                x = g * 8 + h
                drop = jnp.where(top, jnp.broadcast_to(landed[pl.ds(x, 1), :], (128, 128)), 0.0).T
                q[3, x + 2, OWN, :] = q[3, x + 2, OWN, :] + drop
            return 0

        lax.fori_loop(0, X // 8, body, 0)
        dust.start(along_y)
        dust.start(along_x)

    def patch(c):
        def body(x, _):
            q1[c, x + 2, pl.ds(6, 2), :] = yh[0, c, x]
            q1[c, x + 2, pl.ds(136, 2), :] = yh[1, c, x]
            return 0
        lax.fori_loop(0, X, body, 0)

    def keep(c, x, u, value):
        q1[c, x + 2, S(u), :] = value

    def keep_last(c, x, u, value):
        ov[x, S(u), :] = value

    work = (wx, wy, wz, cx, qt, zt, az)
    nothing = lambda j: None

    def edges_come():
        spin.wait_recv(along_x)
        wind.wait_recv(along_x)
        speed_x(0)
        speed_x(X)

    def spin_before(j):
        pl.when(j == PARCELS_AT)(parcels)
        pl.when(j == DEPOSIT_AT)(deposit)
        pl.when(j == PAIRS - 2)(edges_come)

    for c in range(3):
        loads[3 + c].wait()
    spin.wait_recv(along_y)
    sweep(((0, 1, 2),), q, keep, *work, 1, spin_before, nothing)
    for c in range(3):
        second[c].start(along_y)
        second[c].start(along_x)
    dust.wait_recv(along_y)
    sweep(((3,),), q, keep, *work, 1,
          lambda j: pl.when(j == PAIRS - 2)(lambda: dust.wait_recv(along_x)), nothing)
    second[3].start(along_y)
    second[3].start(along_x)
    second[0].wait_recv(along_y)
    patch(0)
    sweep(((0,),), q1, keep_last, *work, 1,
          lambda j: pl.when(j == PAIRS - 2)(lambda: second[0].wait_recv(along_x)), nothing)
    for c in range(1, 4):
        second[c].wait_recv(along_y)
        patch(c)
        second[c].wait_recv(along_x)

    wait_all(packed, 2 * (GX - 1), 0)
    wait_all(rows, GX - 1, 2)
    for exchange in [wind, spin, dust] + second:
        exchange.wait_send()


def second_kernel(q1, wx, wy, wz, ov0, flux_in, out, flux_out, ov, cx, qt, zt, az, osem):
    ready = pltpu.make_async_copy(ov0.at[:, OWN, :], out.at[0], osem.at[1])
    ready.start()
    flux_out[...] = flux_in[...]
    clear_turned(qt)

    def keep(c, x, u, value):
        ov[c - 1, x, S(u), :] = value

    def out_pair(j):
        pltpu.make_async_copy(
            ov.at[:, pl.ds(2 * j, 2), OWN, :], out.at[pl.ds(1, 3), pl.ds(2 * j, 2)], osem.at[0]).start()

    sweep(((1, 2, 3),), q1, keep, wx, wy, wz, cx, qt, zt, az, 0, lambda j: None, out_pair)
    pltpu.make_async_copy(ov.at[:, :, OWN, :], out.at[pl.ds(1, 3)], osem.at[0]).wait()
    ready.wait()


def shards(state, velocity, threshold, tile_owner, parcel_owner, parcel_count, parcel_share):
    def vm(*shape):
        return pltpu.VMEM(shape, f32)

    def like(*shape):
        return jax.ShapeDtypeStruct(shape, f32)

    hbm = pl.BlockSpec(memory_space=pltpu.HBM)

    def far(x):
        return pltpu.with_memory_space_constraint(x, pltpu.HBM)

    vmem = pl.BlockSpec(memory_space=pltpu.VMEM)
    work = [vm(4, 3, 8 * N, 128)] + [vm(8, ROWS, 128)] * 3
    *between, flux = pl.pallas_call(
        first_kernel,
        out_shape=(vm(4, X + 4, ROWS, 128), vm(X + 1, 8 * N, 128), vm(X, 8 * N, 128),
                   vm(X, 8 * N, 128), vm(X, ROWS, 128), like(1, 128)),
        in_specs=[hbm] * 7,
        out_specs=(vmem,) * 6,
        scratch_shapes=[vm(4, X + 4, ROWS, 128), vm(3, X + 2, ROWS, 128), vm(2, 4, X, 2, 128)]
        + work
        + [vm(X, 128), vm(2 * GX, 128), vm(2 * GX, 128), vm(GX, 128), vm(GX, 128),
           vm(1, 128)] + [pltpu.VMEM((1, X), jnp.int32)] * 3 + [vm(X, 128),
           pltpu.SemaphoreType.DMA((12,)), pltpu.SemaphoreType.DMA((7, 4)), pltpu.SemaphoreType.DMA((7, 4)),
           pltpu.SemaphoreType.DMA((4,))],
        compiler_params=pltpu.CompilerParams(
            collective_id=0, has_side_effects=True, vmem_limit_bytes=24 << 20),
    )(*map(far, (state, velocity, threshold, tile_owner.reshape(1, X), parcel_owner.reshape(1, X),
                 parcel_count, parcel_share.reshape(X, 128))))
    return pl.pallas_call(
        second_kernel,
        out_shape=(like(4, X, 128, 128), like(1, 128)),
        in_specs=[vmem] * 6,
        out_specs=(hbm, vmem),
        scratch_shapes=[vm(3, X, ROWS, 128)] + work + [pltpu.SemaphoreType.DMA((2,))],
        compiler_params=pltpu.CompilerParams(vmem_limit_bytes=16 << 20),
    )(*between, flux)


def solution(mesh):
    return jax.shard_map(
        shards,
        mesh=mesh,
        in_specs=(
            P(None, "gx", "gy", None),
            P(None, "gx", "gy", None),
            P("gx", "gy"),
            P("gy", "gx", None),
            P("gy", "gx", None),
            P("gy", "gx"),
            P("gy", "gx", None),
        ),
        out_specs=(P(None, "gx", "gy", None), P("gx", "gy")),
        check_vma=False,
    )
```

time: 55.1 us -> 45.5 us (0.83)
  Pallas kernels: 54.3 us -> 44.7 us
    pallas_call x1, Pallas kernels: 16.9 us -> 11 us  [shards(): pl.pallas_call(second_kernel, out_shape=(like(4, X, 128, 128), like(1, 12...]
    pallas_call x1, Pallas kernels: 37.4 us -> 33.7 us  [shards(): pl.pallas_call(first_kernel, out_shape=(vm(4, X + 4, ROWS, 128), vm(X + 1...]
where the time goes in v2:
time: 45.5 us; the launch traced here: 45.3 us
  Pallas kernels  44.7 us (98%)
  between operations  0.64 us (1%)
    pallas_call x1, Pallas kernels, shards(): pl.pallas_call(first_kernel, out_shape=(vm(4, X + 4, ROWS, 128), vm(X + 1...  33.7 us
    pallas_call x1, Pallas kernels, shards(): pl.pallas_call(second_kernel, out_shape=(like(4, X, 128, 128), like(1, 12...  11 us

profile of v2, /device:TPU:1, one launch (start us, length us, event | category | flops | bytes accessed | tf_op | source)
XLA Modules:
  0.0 45.3 jit_solution(12041763673692710496)
XLA Ops:
  0.6 33.7 %shard_map.86 = (f32[4,36,144,128]{3,2,1,0:T(8,128)S(1)}, f32[33,136,128]{2,1,0:T(8,128)S(1)}, f32[32,136,128]{2,1,0:T(8,128)S(1)}, f32[32,136,128]{2,1,0:T(8,12...) custom-call(f32[4,32,128,128]{3,2,1,0:T(8,128)} %state.1, f32[3,32,128,128]{3,2,1,0:T(8,128)} %vel.1, ...), custom_call_target="tpu_custom_call" | custom-call | tf_op jit(solution)/shard_map/pallas_call | solution.py:541
  34.4 11.0 %shard_map.87 = (f32[4,32,128,128]{3,2,1,0:T(8,128)}, f32[1,128]{1,0:T(1,128)}) custom-call(f32[4,36,144,128]{3,2,1,0:T(8,128)S(1)} %get-tuple-element.8.q1, f32[33,136,128]{2,1,0:T(8,128)S(1)} %get-tuple-element.9.wx, f32[32,136,128]{2,1,0:T(8,128)S(1)} %get-tuple-element.10.wy, f32[32,136,128]{2,1,0:T(8,128)S(1)} %get-tuple-element.11.wz, ...), custom_call_target="tpu_custom_call" | custom-call | tf_op jit(solution)/shard_map/pallas_call | solution.py:557

commit v3 on v2

--- a/solution.py
+++ b/solution.py
@@ -15,7 +15,7 @@
 OWN = pl.ds(8, 128)
 N = 17
 GX, GY = 32, 4
-PARCELS_AT, DEPOSIT_AT = 1, 6
+PARCELS_AT, DEPOSIT_AT = 4, 11
 
 
 def S(k):
@@ -211,12 +211,13 @@
     def local(src, dst, s):
         return pltpu.make_async_copy(src, dst, load_sem.at[s])
 
-    loads = [
-        local(vel.at[a], v.at[a, pl.ds(1, X), OWN, :], a) for a in range(3)
-    ] + [local(state.at[c], q.at[c, pl.ds(2, X), OWN, :], 3 + c) for c in range(4)]
-    loads[0].start()
-    loads[1].start()
-    small = [local(src, dst, 7 + n) for n, (src, dst) in enumerate(
+    def winds(g):
+        return local(vel.at[:, pl.ds(8 * g, 8)], v.at[:, pl.ds(8 * g + 1, 8), OWN, :], g)
+
+    loads = [local(state.at[c], q.at[c, pl.ds(2, X), OWN, :], 4 + c) for c in range(4)]
+    for g in range(X // 8):
+        winds(g).start()
+    small = [local(src, dst, 8 + n) for n, (src, dst) in enumerate(
         ((tile_in, tile), (thr_in, thr), (parcel_in, parcel), (count_in, count), (share_in, share)))]
     for copy in small:
         copy.start()
@@ -260,13 +261,15 @@
         (vel.at[1, :, pl.ds(127, 1), :], v.at[1, pl.ds(1, X), pl.ds(7, 1), :]),
         (vel.at[1, :, pl.ds(0, 1), :], v.at[1, pl.ds(1, X), pl.ds(136, 1), :]),
     ])
-    three = pl.ds(0, 3)
-    spin = Exchange(1, [
-        (state.at[three, pl.ds(X - 2, 2)], q.at[three, pl.ds(0, 2), OWN, :]),
-        (state.at[three, pl.ds(0, 2)], q.at[three, pl.ds(X + 2, 2), OWN, :]),
-        (state.at[three, :, pl.ds(126, 2), :], q.at[three, all_x, pl.ds(6, 2), :]),
-        (state.at[three, :, pl.ds(0, 2), :], q.at[three, all_x, pl.ds(136, 2), :]),
-    ])
+    spin = [
+        Exchange(7 + c, [
+            (state.at[c, pl.ds(X - 2, 2)], q.at[c, pl.ds(0, 2), OWN, :]),
+            (state.at[c, pl.ds(0, 2)], q.at[c, pl.ds(X + 2, 2), OWN, :]),
+            (state.at[c, :, pl.ds(126, 2), :], q.at[c, all_x, pl.ds(6, 2), :]),
+            (state.at[c, :, pl.ds(0, 2), :], q.at[c, all_x, pl.ds(136, 2), :]),
+        ])
+        for c in range(3)
+    ]
     dust = Exchange(2, [
         (q.at[3, pl.ds(X, 2), OWN, :], q.at[3, pl.ds(0, 2), OWN, :]),
         (q.at[3, pl.ds(2, 2), OWN, :], q.at[3, pl.ds(X + 2, 2), OWN, :]),
@@ -323,23 +326,55 @@
     pl.when(gy == 0)(lambda: clear_rows(0, 6, 7))
     pl.when(gy == GY - 1)(lambda: clear_rows(1, 136, 136))
 
-    loads[0].wait()
-    loads[1].wait()
-    for copy in loads[2:]:
-        copy.start()
-
-    def friction(g, _):
+    pl.semaphore_wait(
+        barrier, GX - 1 + source[2].astype(jnp.int32) + source[3].astype(jnp.int32))
+    wind.start(along_y)
+    for c in range(3):
+        spin[c].start(along_y)
+
+
+    def below(k):
+        return pl.ds(3 + k, 8, stride=N)
+
+    def speed_x(i):
+        for k in range(N):
+            wx[i, A(k), :] = SCALE * (v[0, i, S(k), :] + v[0, i + 1, S(k), :])
+
+    def speed_y(i, ks):
+        for k in ks:
+            wy[i, A(k), :] = SCALE * (v[1, i + 1, below(k), :] + v[1, i + 1, S(k), :])
+
+    beside = (3, 4, 13, 14)
+
+    def local_work(g, _):
+        winds(g).wait()
+
+        @pl.when(g == 1)
+        def _():
+            for copy in loads:
+                copy.start()
+
         for h in range(8):
             x = g * 8 + h
+            qt[h, OWN, :] = v[2, x + 1, OWN, :].T
             east, north = v[0, x + 1, OWN, :], v[1, x + 1, OWN, :]
             levels = (east * east + north * north).T
             total = profile_weights[0] * levels[0:1]
             for level in range(1, 4):
                 total = total + profile_weights[level] * levels[level:level + 1]
             stress[pl.ds(x, 1), :] = total
+        for h in range(8):
+            x = g * 8 + h
+            speed_y(x, [k for k in range(N) if k not in beside])
+            if h:
+                speed_x(x)
+            for k in range(N):
+                wz[x, A(k), :] = SCALE * (qt[h, below(k), :] + qt[h, S(k), :])
         return 0
 
-    lax.fori_loop(0, X // 8, friction, 0)
+    lax.fori_loop(0, X // 8, local_work, 0)
+    for x in range(8, X, 8):
+        speed_x(x)
 
     def column(row):
         spot = lax.broadcasted_iota(jnp.int32, (X, X), 0) == lax.broadcasted_iota(jnp.int32, (X, X), 1)
@@ -382,46 +417,20 @@
         part = ref.at[pl.ds(0, count), :]
         pltpu.make_async_copy(part, part, a2a_sem.at[s]).wait()
 
-    pl.semaphore_wait(
-        barrier, GX - 1 + source[2].astype(jnp.int32) + source[3].astype(jnp.int32))
     send_all(tiles_to)
-    wind.start(along_y)
-    spin.start(along_y)
-    spin.start(along_x)
+    for c in range(3):
+        spin[c].start(along_x)
     wind.start(along_x)
     got[pl.ds(2 * gx, 2), :] = packed[pl.ds(2 * gx, 2), :]
 
-    def speed_x(i):
-        for k in range(N):
-            wx[i, A(k), :] = SCALE * (v[0, i, S(k), :] + v[0, i + 1, S(k), :])
-
-    def speeds_x(i, _):
-        speed_x(i)
+    wind.wait_recv(along_y)
+
+    def speeds_y(g, _):
+        for h in range(8):
+            speed_y(g * 8 + h, beside)
         return 0
 
-    lax.fori_loop(1, X, speeds_x, 0)
-    loads[2].wait()
-
-    def below(k):
-        return pl.ds(3 + k, 8, stride=N)
-
-    def speeds_z(g, _):
-        for b in range(8):
-            qt[b, OWN, :] = v[2, g * 8 + b + 1, OWN, :].T
-        for b in range(8):
-            for k in range(N):
-                wz[g * 8 + b, A(k), :] = SCALE * (qt[b, below(k), :] + qt[b, S(k), :])
-        return 0
-
-    lax.fori_loop(0, X // 8, speeds_z, 0)
-    wind.wait_recv(along_y)
-
-    def speeds_y(i, _):
-        for k in range(N):
-            wy[i, A(k), :] = SCALE * (v[1, i + 1, below(k), :] + v[1, i + 1, S(k), :])
-        return 0
-
-    lax.fori_loop(0, X, speeds_y, 0)
+    lax.fori_loop(0, X // 8, speeds_y, 0)
 
     def parcels():
         wait_all(got, 2 * (GX - 1), 1)
@@ -438,7 +447,7 @@
 
     def deposit():
         wait_all(landed, GX - 1, 3)
-        loads[6].wait()
+        loads[3].wait()
         top = lax.broadcasted_iota(jnp.int32, (128, 128), 0) == 0
 
         def body(g, _):
@@ -469,7 +478,8 @@
     nothing = lambda j: None
 
     def edges_come():
-        spin.wait_recv(along_x)
+        for c in range(3):
+            spin[c].wait_recv(along_x)
         wind.wait_recv(along_x)
         speed_x(0)
         speed_x(X)
@@ -480,8 +490,8 @@
         pl.when(j == PAIRS - 2)(edges_come)
 
     for c in range(3):
-        loads[3 + c].wait()
-    spin.wait_recv(along_y)
+        loads[c].wait()
+        spin[c].wait_recv(along_y)
     sweep(((0, 1, 2),), q, keep, *work, 1, spin_before, nothing)
     for c in range(3):
         second[c].start(along_y)
@@ -502,7 +512,7 @@
 
     wait_all(packed, 2 * (GX - 1), 0)
     wait_all(rows, GX - 1, 2)
-    for exchange in [wind, spin, dust] + second:
+    for exchange in [wind, dust] + spin + second:
         exchange.wait_send()
 
 
@@ -548,7 +558,7 @@
         + work
         + [vm(X, 128), vm(2 * GX, 128), vm(2 * GX, 128), vm(GX, 128), vm(GX, 128),
            vm(1, 128)] + [pltpu.VMEM((1, X), jnp.int32)] * 3 + [vm(X, 128),
-           pltpu.SemaphoreType.DMA((12,)), pltpu.SemaphoreType.DMA((7, 4)), pltpu.SemaphoreType.DMA((7, 4)),
+           pltpu.SemaphoreType.DMA((13,)), pltpu.SemaphoreType.DMA((10, 4)), pltpu.SemaphoreType.DMA((10, 4)),
            pltpu.SemaphoreType.DMA((4,))],
         compiler_params=pltpu.CompilerParams(
             collective_id=0, has_side_effects=True, vmem_limit_bytes=24 << 20),

time: 45.5 us -> 44.2 us (0.971)
  Pallas kernels: 44.7 us -> 43.4 us
    pallas_call x1, Pallas kernels: 33.7 us -> 32.4 us  [shards(): pl.pallas_call(first_kernel, out_shape=(vm(4, X + 4, ROWS, 128), vm(X + 1...]
where the time goes in v3:
time: 44.2 us; the launch traced here: 44 us
  Pallas kernels  43.4 us (98%)
  between operations  0.64 us (1%)
    pallas_call x1, Pallas kernels, shards(): pl.pallas_call(first_kernel, out_shape=(vm(4, X + 4, ROWS, 128), vm(X + 1...  32.4 us
    pallas_call x1, Pallas kernels, shards(): pl.pallas_call(second_kernel, out_shape=(like(4, X, 128, 128), like(1, 12...  11 us

profile of v3, /device:TPU:1, one launch (start us, length us, event | category | flops | bytes accessed | tf_op | source)
XLA Modules:
  0.0 44.0 jit_solution(9018872065289250961)
XLA Ops:
  0.6 32.4 %shard_map.86 = (f32[4,36,144,128]{3,2,1,0:T(8,128)S(1)}, f32[33,136,128]{2,1,0:T(8,128)S(1)}, f32[32,136,128]{2,1,0:T(8,128)S(1)}, f32[32,136,128]{2,1,0:T(8,12...) custom-call(f32[4,32,128,128]{3,2,1,0:T(8,128)} %state.1, f32[3,32,128,128]{3,2,1,0:T(8,128)} %vel.1, ...), custom_call_target="tpu_custom_call" | custom-call | tf_op jit(solution)/shard_map/pallas_call | solution.py:551
  33.1 11.0 %shard_map.87 = (f32[4,32,128,128]{3,2,1,0:T(8,128)}, f32[1,128]{1,0:T(1,128)}) custom-call(f32[4,36,144,128]{3,2,1,0:T(8,128)S(1)} %get-tuple-element.8.q1, f32[33,136,128]{2,1,0:T(8,128)S(1)} %get-tuple-element.9.wx, f32[32,136,128]{2,1,0:T(8,128)S(1)} %get-tuple-element.10.wy, f32[32,136,128]{2,1,0:T(8,128)S(1)} %get-tuple-element.11.wz, ...), custom_call_target="tpu_custom_call" | custom-call | tf_op jit(solution)/shard_map/pallas_call | solution.py:567
